TPU v7x, 256 devices: a whole 4x4x8 slice. The times are simulated.
256 devices in a mesh: dp: 128 (over x, y_lo, z, core), fsdp: 2 (over y_hi).
Axes of the slice: x: 4, y: 4 (y_hi: 2, y_lo: 2; y = y_hi * 2 + y_lo), z: 8, core: 2. Of those that a mesh axis runs over, the one named last changes fastest.
Arguments:
- img_feat: bfloat16 [8192, 1408], P('dp'), may hold values from -64 to 64
- txt_feat: bfloat16 [8192, 1408], P('dp'), may hold values from -64 to 64
- img_weight: bfloat16 [1408, 1536], P(None, 'fsdp'), may hold values from -2 to 2
- txt_weight: bfloat16 [1408, 1536], P(None, 'fsdp'), may hold values from -2 to 2
- logit_scale: float32 [1], replicated, may hold values from 30 to 60
- logit_bias: float32 [1], replicated, may hold values from -9 to -6
Outputs:
- loss: float32 [], replicated
- img_feat_grad: float32 [8192, 1408], P('dp', 'fsdp')
- txt_feat_grad: float32 [8192, 1408], P('dp', 'fsdp')
- txt_weight_grad: float32 [1408, 1536], P('dp', 'fsdp')
All inputs are finite; a program needn't handle non-finite values.
Results may differ from a plain program's by a relative error of at most 0.0031.
Values may be sent and summed in bfloat16 or wider, within the bound.
A program may use at most 128 MiB of HBM per device.

v0:
```python
import jax
import jax.numpy as jnp
from jax import lax
from jax.sharding import PartitionSpec as P

EPS = 1e-06


def from_partner(value, axis, apart):
    mask = 2**apart
    pairs = [(source, source ^ mask) for source in range(lax.axis_size(axis))]
    return lax.ppermute(value, axis, pairs)


def sigmoid_terms(query_units, block_keys, row_start, scale_value, bias_value):
    logits = (
        scale_value * jnp.dot(query_units, block_keys.T, preferred_element_type=jnp.float32)
        + bias_value
    )
    row_ids = row_start + jnp.arange(query_units.shape[0], dtype=jnp.int32)[:, None]
    col_ids = jnp.arange(block_keys.shape[0], dtype=jnp.int32)[None, :]
    label_sign = jnp.where(row_ids == col_ids, 1.0, -1.0).astype(jnp.float32)
    summed = jnp.sum(jax.nn.softplus(-label_sign * logits))
    slope = (-label_sign * jax.nn.sigmoid(-label_sign * logits) * scale_value).astype(jnp.bfloat16)
    return (jnp.dot(slope, block_keys, preferred_element_type=jnp.float32), summed)


def body(img_feat, txt_feat, img_weight, txt_weight, logit_scale, logit_bias):
    batch_rows = img_feat.shape[0]
    half_cols = img_weight.shape[1]
    fsdp_index = lax.axis_index("fsdp")
    dp_index = lax.axis_index("dp")
    scale_value = logit_scale[0]
    bias_value = logit_bias[0]
    features = jnp.stack([img_feat, txt_feat])
    weights = jnp.stack([img_weight, txt_weight])
    own_part = jnp.einsum("mbf,mfe->mbe", features, weights, preferred_element_type=jnp.float32)
    projected = lax.all_gather(own_part, "fsdp", axis=2, tiled=True)
    norm_rows = jnp.sqrt(jnp.sum(projected * projected, axis=2, keepdims=True) + EPS)
    unit_rows = projected / norm_rows
    unit_emb = unit_rows.astype(jnp.bfloat16)
    row_base = dp_index * batch_rows
    leading = fsdp_index == 0
    query_units = jnp.where(leading, unit_emb[0], unit_emb[1])
    key_units = jnp.where(leading, unit_emb[1], unit_emb[0])
    grad_part, summed = sigmoid_terms(
        query_units,
        lax.all_gather(key_units, "dp", axis=0, tiled=True),
        row_base,
        scale_value,
        bias_value,
    )
    partner = from_partner(grad_part, "fsdp", 0)
    unit_grad = jnp.stack(
        [jnp.where(leading, grad_part, partner), jnp.where(leading, partner, grad_part)]
    )
    loss_share = 0.5
    loss_value = lax.psum(summed, ("dp", "fsdp")) * loss_share / (batch_rows * lax.axis_size("dp"))
    inner = jnp.sum(unit_rows * unit_grad, axis=2, keepdims=True)
    proj_grad = ((unit_grad - unit_rows * inner) / norm_rows).astype(jnp.bfloat16)
    own_grad = lax.dynamic_slice_in_dim(proj_grad, fsdp_index * half_cols, half_cols, 2)
    feature_terms = jnp.einsum(
        "mbe,mfe->mbf", own_grad, weights, preferred_element_type=jnp.float32
    )
    feature_grads = lax.psum_scatter(feature_terms, "fsdp", scatter_dimension=2, tiled=True)
    text_grad = own_grad[1]
    weight_grads = lax.psum_scatter(
        jnp.dot(txt_feat.T, text_grad, preferred_element_type=jnp.float32),
        "dp",
        scatter_dimension=0,
        tiled=True,
    )
    return (loss_value, feature_grads[0], feature_grads[1], weight_grads)


def solution(mesh):
    placed = (P("dp", None), P("dp", None), P(None, "fsdp"), P(None, "fsdp"), P(), P())
    return jax.shard_map(
        body,
        mesh=mesh,
        in_specs=placed,
        out_specs=(P(), P("dp", "fsdp"), P("dp", "fsdp"), P("dp", "fsdp")),
        check_vma=False,
    )
```

profile of v0, /device:TPU:1, one launch (start us, length us, event | category | flops | bytes accessed | tf_op | source)
XLA Modules:
  0.0 1416.1 jit_solution(5131321531292139080)
XLA Ops:
  7.2 0.0 all-gather.3.cloned.1.call-start
  7.2 3.3 fusion.14
  10.5 12.2 all_gather.6
  22.7 0.1 multiply_reduce_fusion
  22.9 0.2 fusion.38
  23.1 0.7 broadcast_select_fusion
  23.8 0.0 all-gather.3.cloned.1.call-update
  23.8 0.0 reduce-scatter.5.cloned.1.call-start
  25.2 245.5 %all-gather.3.cloned.1.call-done = bf16[1,8192,1536]{2,1,0:T(8,128)(2,1)} async-done(((bf16[1,64,1536]{2,1,0:T(8,128)(2,1)}), bf16[1,8192,1536]{2,1,0:T(8,128)(2,1)}) %all-gather.3.cloned.1.call-update) | async-done | bytes 25165840 | tf_op jit(solution)/shard_map/all_gather | solution.py:48
  270.6 13.2 fusion.15
  283.8 10.6 fusion
  294.4 3.0 collective-permute-start
  297.4 0.0 copy-start.1
  297.4 0.0 copy-start.2
  297.4 8.1 collective-permute-done
  305.5 0.1 select_bitcast_fusion.1
  305.6 0.2 fusion.21
  305.7 0.1 fusion.25
  305.9 0.0 copy-done.1
  305.9 0.0 copy-done.2
  305.9 1.4 fusion.13
  307.3 0.0 copy-start
  307.3 1.4 copy.12
  308.7 1.7 reshape.25
  310.5 0.0 reduce-scatter.5.cloned.1.call-update
  310.5 0.0 all-reduce.3.cloned.1.call-start
  310.5 0.0 copy-done
  310.6 2.8 convolution_bitcast_fusion
  313.3 0.0 copy-start.3
  313.3 0.0 all-reduce.3.cloned.1.call-update
  313.4 0.6 copy-done.3
  314.0 0.6 dynamic-slice
  315.2 80.1 %psum.7 = f32[]{:T(128)} all-reduce(f32[]{:T(128)} %get-tuple-element.18), channel_id=1, replica_groups=mesh['dp'=128,'fsdp'=2] {'dp','fsdp'}, use_global_device_ids=true, to_apply=%region_2.3 | all-reduce | flops 1 | bytes 8 | tf_op jit(solution)/shard_map/psum | solution.py:58
  396.0 0.0 reduce-scatter.5.cloned.1.call-done
  396.1 1.4 reshape.26
  397.5 0.6 fusion.39
  398.0 0.8 copy.16
  398.9 0.8 copy.17
  399.7 1006.7 %all-reduce.3.cloned.1.call-done = f32[1408,768]{0,1:T(8,128)} async-done(((f32[1408,768]{0,1:T(8,128)}), f32[1408,768]{0,1:T(8,128)}) %all-reduce.3.cloned.1.call-update) | async-done | bytes 4325392
  1406.4 1.3 constant_dynamic-slice_fusion
  1407.7 0.8 copy.11
  (2 shorter events, 0.0 us)
Async XLA Ops:
  7.2 263.5 %all-gather.3.cloned.1.call-start = ((), (), s32[]{:S(2)}) async-start(), calls=%async_computation.1 | async-start | bytes 25362432 | tf_op jit(solution)/shard_map/all_gather | solution.py:48
  23.8 372.3 %reduce-scatter.5.cloned.1.call-start = ((), (), s32[]{:S(2)}) async-start(), calls=%async_computation.2 | async-start | bytes 1081344
  294.4 11.1 collective-permute-start
  297.4 8.5 copy-start.1
  297.4 8.5 copy-start.2
  307.3 3.3 copy-start
  310.5 1095.9 %all-reduce.3.cloned.1.call-start = ((), (), s32[]{:S(2)}) async-start(), calls=%async_computation.3 | async-start | bytes 8650752
  313.3 0.7 copy-start.3
Sparse Core Ops, SparseCore 0:
  23.9 246.6 all-gather.2
  310.6 24.8 reduce-scatter.4
  338.3 1068.0 all-reduce.2
where the time goes:
time: 1420 us
  waiting for transfers between devices  1260 us (89%)
  blocking collectives  92.3 us (6%)
  matrix products  31.2 us (2%)
  between operations  17.6 us (1%)
    unnamed x5, waiting for transfers between devices  1010 us
    all_gather x1, waiting for transfers between devices, body(): lax.all_gather(key_units, 'dp', axis=0, tiled=True)  245 us
    psum x1, blocking collectives, body(): lax.psum(summed, ('dp', 'fsdp')) * loss_share  80.1 us
  transfers between devices with their start and end apart: 4, of which 3 were waited for; matrix products, arithmetic and copies ran while one was open for 0% of the time, Pallas kernels for 0%

commit v1 on v0

v1 whole, which is shorter than its diff:
```python
import jax
import jax.numpy as jnp
from jax import lax
from jax.experimental import pallas as pl
from jax.experimental.pallas import tpu as pltpu
from jax.sharding import PartitionSpec as P

EPS = 1e-06
MESH = pl.DeviceIdType.MESH
BF = jnp.bfloat16
F32 = jnp.float32
R = 32
E = 1536
H = 768
FEAT = 1408
FH = 704
N_SEM = 112


def dot_nt(a, b):
    return lax.dot_general(a, b, (((1,), (1,)), ((), ())), preferred_element_type=F32)


def dot_tn(a, b):
    return lax.dot_general(a, b, (((0,), (0,)), ((), ())), preferred_element_type=F32)


def kernel(
    scale_ref, bias_ref, img_feat, txt_feat, img_w_hbm, txt_w_hbm,
    loss_out, img_out, txt_out, wg_out,
    w_img, w_txt, proj, proj_rcv, full, norms,
    txt_all, img_all, slope_s, feat_win,
    a_send, a_rcv, a_own, a2_send, a2_rcv,
    b_send, b_rcv, b_own, b2_send, b2_rcv,
    ci_send, ci_rcv, pi_own, zp_send, zp_rcv, zm_send, zm_rcv,
    pgf, pg64, pgx, fg_send, fg_rcv,
    wg, cw_send, cw_rcv, y_send, y_rcv, s2, zw_rcv,
    lx, ly, lc, lz, loss_v,
    ssem, rsem, wsem,
):
    dp = lax.axis_index("dp")
    yh = lax.axis_index("fsdp")
    c = lax.rem(dp, 2)
    z = lax.rem(dp // 2, 8)
    yl = lax.rem(dp // 16, 2)
    x = dp // 32
    y = yh * 2 + yl

    def dev(x_, y_, z_, c_):
        return {"dp": ((x_ * 2 + lax.rem(y_, 2)) * 8 + z_) * 2 + c_, "fsdp": y_ // 2}

    def dx(k):
        return dev(lax.rem(x + k, 4), y, z, c)

    def dy(k):
        return dev(x, lax.rem(y + k, 4), z, c)

    def dz(k):
        return dev(x, y, lax.rem(z + k, 8), c)

    other = dev(x, y, z, 1 - c)
    fs_partner = dy(2)
    yl_partner = dev(x, yh * 2 + (1 - yl), z, c)

    counter = [0]

    def copy(src, dst, target):
        i = counter[0]
        counter[0] += 1
        cp = pltpu.make_async_remote_copy(
            src_ref=src, dst_ref=dst, send_sem=ssem.at[i], recv_sem=rsem.at[i],
            device_id=target, device_id_type=MESH,
        )
        cp.start()
        sent.append(cp)
        return cp

    sent = []

    load_txt = pltpu.make_async_copy(txt_w_hbm, w_txt, wsem.at[0])
    load_img = pltpu.make_async_copy(img_w_hbm, w_img, wsem.at[1])
    load_txt.start()
    load_img.start()

    barrier = pltpu.get_barrier_semaphore()
    partners = [dx(k) for k in (1, 2, 3)] + [dy(k) for k in (1, 2, 3)]
    partners += [dz(k) for k in range(1, 8)] + [other]
    for p in partners:
        pl.semaphore_signal(barrier, inc=1, device_id=p, device_id_type=MESH)

    mine = pl.ds(pl.multiple_of(yh * R, R), R)
    theirs = pl.ds(pl.multiple_of((1 - yh) * R, R), R)
    my_cols = pl.ds(pl.multiple_of(yh * H, 128), H)
    their_cols = pl.ds(pl.multiple_of((1 - yh) * H, 128), H)

    load_txt.wait()
    proj[1] = jnp.dot(txt_feat[...], w_txt[...], preferred_element_type=F32)
    pl.semaphore_wait(barrier, len(partners))
    swap_txt = copy(proj.at[1, theirs], proj_rcv.at[1], fs_partner)
    load_img.wait()
    proj[0] = jnp.dot(img_feat[...], w_img[...], preferred_element_type=F32)
    swap_img = copy(proj.at[0, theirs], proj_rcv.at[0], fs_partner)

    def window(x_):
        return pl.ds(pl.multiple_of(256 * x_ + 128 * (x_ // 2), 128), 512)

    feat_win[0] = txt_feat[:, window(x)]

    def embed(m):
        own = proj[m, mine, :]
        got = proj_rcv[m]
        total = jnp.sum(own * own, axis=1, keepdims=True) + jnp.sum(got * got, axis=1, keepdims=True)
        norm = jnp.sqrt(total + EPS)
        norms[m] = jnp.broadcast_to(norm, (R, 128))
        full[m, :, my_cols] = own / norm
        full[m, :, their_cols] = got / norm
        return full[m].astype(BF)

    A = pl.ds(0, H)
    B = pl.ds(H, H)

    swap_txt.wait_recv()
    txt_all[0, 0] = embed(1)
    ax = {}
    ay = {}
    bx = {}
    by = {}
    for k in (1, 3, 2):
        ax[k] = copy(txt_all.at[0, 0, :, A], txt_all.at[4 - k, 0, :, A], dx(k))
        by[k] = copy(txt_all.at[0, 0, :, B], txt_all.at[0, 4 - k, :, B], dy(k))
    swap_img.wait_recv()
    img_all[0, 0] = embed(0)
    zp = {}
    zm = {}
    cf = {}
    zp[1] = copy(img_all.at[0, 0], img_all.at[0, 7], dz(1))
    zm[1] = copy(img_all.at[0, 0], img_all.at[0, 1], dz(7))
    cf[0] = copy(img_all.at[0, 0], img_all.at[1, 0], other)
    for k in (1, 3, 2):
        ay[0, k] = copy(txt_all.at[0, 0, :, A], txt_all.at[0, 4 - k, :, A], dy(k))
        bx[0, k] = copy(txt_all.at[0, 0, :, B], txt_all.at[4 - k, 0, :, B], dx(k))

    def second(k):
        slot = 4 - k
        ax[k].wait_recv()
        for j in (1, 3, 2):
            ay[slot, j] = copy(txt_all.at[slot, 0, :, A], txt_all.at[slot, 4 - j, :, A], dy(j))
        by[k].wait_recv()
        for j in (1, 3, 2):
            bx[slot, j] = copy(txt_all.at[0, slot, :, B], txt_all.at[4 - j, slot, :, B], dx(j))

    second(1)
    second(3)
    for step in (1, 2):
        zp[step].wait_recv()
        zp[step + 1] = copy(img_all.at[0, 8 - step], img_all.at[0, 7 - step], dz(1))
        cf[8 - step] = copy(img_all.at[0, 8 - step], img_all.at[1, 8 - step], other)
        zm[step].wait_recv()
        zm[step + 1] = copy(img_all.at[0, step], img_all.at[0, step + 1], dz(7))
        cf[step] = copy(img_all.at[0, step], img_all.at[1, step], other)
        if step == 1:
            second(2)
    zp[3].wait_recv()
    zp[4] = copy(img_all.at[0, 5, :, A], img_all.at[0, 4, :, A], dz(1))
    cf[5] = copy(img_all.at[0, 5], img_all.at[1, 5], other)
    zm[3].wait_recv()
    zm[4] = copy(img_all.at[0, 3, :, B], img_all.at[0, 4, :, B], dz(7))
    cf[3] = copy(img_all.at[0, 3], img_all.at[1, 3], other)
    zp[4].wait_recv()
    zm[4].wait_recv()
    cf[4] = copy(img_all.at[0, 4], img_all.at[1, 4], other)
    for s in range(4):
        for j in (1, 2, 3):
            ay[s, j].wait_recv()
            bx[s, j].wait_recv()
    for s in range(8):
        cf[s].wait_recv()

    fw = [copy(txt_feat.at[:, window(lax.rem(x + k, 4))], feat_win.at[4 - k], dx(k)) for k in (1, 2, 3)]

    scale = scale_ref[0]
    bias = bias_ref[0]
    txt_rows = txt_all[...].reshape(16 * R, E)
    loss_v[...] = jnp.zeros_like(loss_v)

    def tile(i, carry):
        row0 = pl.multiple_of(i * 4, 4)
        rows = img_all[i // 2, pl.ds(pl.multiple_of((i % 2) * 4, 4), 4)].reshape(4 * R, E)
        logits = scale * dot_nt(rows, txt_rows) + bias
        ri = lax.broadcasted_iota(jnp.int32, logits.shape, 0) + i * (4 * R)
        ci = lax.broadcasted_iota(jnp.int32, logits.shape, 1)
        label = jnp.where((ri == ci) & (ri < R), 1.0, -1.0).astype(F32)
        v = -label * logits
        t = jnp.exp(-jnp.abs(v))
        loss_v[...] += jnp.sum((jnp.maximum(v, 0.0) + jnp.log1p(t)).reshape(16, 8, 16 * R), axis=0)
        sig = jnp.where(v >= 0, 1.0, t) / (1.0 + t)
        slope_s[pl.ds(pl.multiple_of(i * 4 * R, 4 * R), 4 * R), :] = (-label * sig * scale).astype(BF)
        return carry

    lax.fori_loop(0, 4, tile, 0)

    img_rows = img_all[...].reshape(16 * R, E)
    sa = {}
    for k in (1, 3, 2, 0):
        g = dot_tn(slope_s[:, k * 128:(k + 1) * 128], img_rows)
        ga = g[:, :H].reshape(4, R, H)
        gb = g[:, H:].reshape(4, R, H)
        if k:
            a_send[k - 1] = ga.astype(BF)
            sa[k] = copy(a_send.at[k - 1], a_rcv.at[3 - k], dx(k))
        else:
            a_own[...] = ga
        b_own[k] = gb[0]
        for j in (1, 2, 3):
            b_send[j - 1, k] = gb[j].astype(BF)
    sb = {}
    for j in (1, 3, 2):
        sb[j] = copy(b_send.at[j - 1], b_rcv.at[3 - j], dy(j))

    ci_send[...] = jnp.dot(
        slope_s[8 * R:, :], txt_rows, preferred_element_type=F32
    ).astype(BF).reshape(8, R, E)
    ci_copy = copy(ci_send, ci_rcv, other)
    pi_own[...] = jnp.dot(slope_s[:8 * R, :], txt_rows, preferred_element_type=F32).reshape(8, R, E)

    part = jnp.sum(loss_v[...])
    lx[0] = jnp.full((8, 128), part, F32)
    lxc = [copy(lx.at[0], lx.at[4 - k], dx(k)) for k in (1, 2, 3)]

    ci_copy.wait_recv()
    pi_own[...] += ci_rcv[...].astype(F32)

    zp_send[0] = pi_own[4].astype(BF)
    rzp = [copy(zp_send.at[0, :, A], zp_rcv.at[0, :, A], dz(1))]
    rzm = [copy(zp_send.at[0, :, B], zm_rcv.at[0, :, B], dz(7))]

    def ring(step):
        rzp[step - 1].wait_recv()
        rzm[step - 1].wait_recv()
        if step == 1:
            zp_send[1, :, A] = (pi_own[3, :, A] + zp_rcv[0, :, A].astype(F32)).astype(BF)
            zp_send[1, :, B] = pi_own[3, :, B].astype(BF)
            zm_send[1, :, B] = (pi_own[5, :, B] + zm_rcv[0, :, B].astype(F32)).astype(BF)
            zm_send[1, :, A] = pi_own[5, :, A].astype(BF)
        else:
            zp_send[step] = (pi_own[4 - step] + zp_rcv[step - 1].astype(F32)).astype(BF)
            zm_send[step] = (pi_own[4 + step] + zm_rcv[step - 1].astype(F32)).astype(BF)
        rzp.append(copy(zp_send.at[step], zp_rcv.at[step], dz(1)))
        rzm.append(copy(zm_send.at[step], zm_rcv.at[step], dz(7)))

    ring(1)

    for k in (1, 2, 3):
        sa[k].wait_recv()
    ga = a_own[...] + a_rcv[0].astype(F32) + a_rcv[1].astype(F32) + a_rcv[2].astype(F32)
    a2_send[...] = ga[1:].astype(BF)
    a2 = [copy(a2_send.at[k - 1], a2_rcv.at[3 - k], dy(k)) for k in (1, 2, 3)]
    for k in (1, 2, 3):
        sb[k].wait_recv()
    gb = b_own[...] + b_rcv[0].astype(F32) + b_rcv[1].astype(F32) + b_rcv[2].astype(F32)
    b2_send[...] = gb[1:].astype(BF)
    b2 = [copy(b2_send.at[k - 1], b2_rcv.at[3 - k], dx(k)) for k in (1, 2, 3)]
    ga0 = ga[0]
    gb0 = gb[0]

    for cp in lxc:
        cp.wait_recv()
    ly[0] = (lx[0] + lx[2]) + (lx[1] + lx[3])
    lyc = [copy(ly.at[0], ly.at[4 - k], dy(k)) for k in (1, 2, 3)]

    ring(2)

    for cp in a2:
        cp.wait_recv()
    for cp in b2:
        cp.wait_recv()
    ga0 = ga0 + a2_rcv[0].astype(F32) + a2_rcv[1].astype(F32) + a2_rcv[2].astype(F32)
    gb0 = gb0 + b2_rcv[0].astype(F32) + b2_rcv[1].astype(F32) + b2_rcv[2].astype(F32)

    def back(m, ga, gb):
        ua = full[m, :, A]
        ub = full[m, :, B]
        inner = jnp.sum(ua * ga, axis=1, keepdims=True) + jnp.sum(ub * gb, axis=1, keepdims=True)
        norm = norms[m, :, 0:1]
        pgf[m, :, A] = ((ga - ua * inner) / norm).astype(BF)
        pgf[m, :, B] = ((gb - ub * inner) / norm).astype(BF)
        cp = copy(pgf.at[m, :, their_cols], pg64.at[m, mine], fs_partner)
        pg64[m, mine, :] = pgf[m, :, my_cols]
        return cp

    pg_txt = back(1, ga0, gb0)
    ring(3)
    pg_txt.wait_recv()
    pgx[0] = pg64[1]
    px = [copy(pg64.at[1], pgx.at[4 - k], dx(k)) for k in (1, 3, 2)]

    my_feat = pl.ds(pl.multiple_of(yh * FH, 16), FH)
    their_feat = pl.ds(pl.multiple_of((1 - yh) * FH, 16), FH)

    def feature_terms(m, w):
        fg_send[m] = dot_nt(pg64[m], w[their_feat, :])
        cp = copy(fg_send.at[m], fg_rcv.at[m], fs_partner)
        return cp

    fg_txt = feature_terms(1, w_txt)
    txt_out[...] = dot_nt(pg64[1], w_txt[my_feat, :])

    for cp in lyc:
        cp.wait_recv()
    lc[0] = (ly[0] + ly[2]) + (ly[1] + ly[3])
    lcc = copy(lc.at[0], lc.at[1], other)

    for cp in fw:
        cp.wait_recv()
    for cp in px:
        cp.wait_recv()
    wg[0:512, :] = dot_tn(feat_win[...].reshape(4 * 64, 512), pgx[...].reshape(4 * 64, H))
    wg[512:528, :] = jnp.zeros((16, H), F32)
    start = 352 * x - (256 * x + 128 * (x // 2))

    def rows16(k, core):
        first = start + 22 * k + 11 * core
        low = first // 8
        block = wg[pl.ds(pl.multiple_of(low * 8, 8), 24), :]
        return pltpu.roll(block, 24 - (first - low * 8), 0)[:16]

    def cut(k, carry):
        cw_send[k] = rows16(k, 1 - c).astype(BF)
        return carry

    lax.fori_loop(0, 16, cut, 0)
    cw = copy(cw_send, cw_rcv, other)

    rzp[3].wait_recv()
    rzm[3].wait_recv()
    gi = pi_own[0] + zp_rcv[3].astype(F32) + zm_rcv[3].astype(F32)
    pg_img = back(0, gi[:, :H], gi[:, H:])

    cw.wait_recv()

    def add_core(k, carry):
        kk = (1 - yl) * 8 + k
        y_send[k] = (
            rows16(kk, c) + cw_rcv[kk].astype(F32)
        ).astype(BF)
        return carry

    lax.fori_loop(0, 8, add_core, 0)
    yw = copy(y_send, y_rcv, yl_partner)

    lcc.wait_recv()
    lz[0] = lc[0] + lc[1]
    lzc = [copy(lz.at[0], lz.at[8 - k], dz(k)) for k in range(1, 8)]

    pg_img.wait_recv()
    fg_img = feature_terms(0, w_img)
    img_out[...] = dot_nt(pg64[0], w_img[my_feat, :])

    yw.wait_recv()

    def add_y(k, carry):
        kk = yl * 8 + k
        s2[k] = (
            rows16(kk, c) + cw_rcv[kk].astype(F32) + y_rcv[k].astype(F32)
        ).astype(BF)
        return carry

    lax.fori_loop(0, 8, add_y, 0)
    zw = [copy(s2.at[lax.rem(z + k, 8)], zw_rcv.at[7 - k], dz(k)) for k in (1, 7, 2, 6, 3, 5, 4)]
    own_w = (
        rows16(yl * 8 + z, c) + cw_rcv[yl * 8 + z].astype(F32) + y_rcv[z].astype(F32)
    )

    fg_txt.wait_recv()
    txt_out[...] += fg_rcv[1]
    for cp in lzc:
        cp.wait_recv()
    total = ((lz[0] + lz[4]) + (lz[2] + lz[6])) + ((lz[1] + lz[5]) + (lz[3] + lz[7]))
    loss_out[...] = total / 8192.0
    for cp in zw:
        cp.wait_recv()
    for k in range(7):
        own_w = own_w + zw_rcv[k].astype(F32)
    wg_out[...] = own_w[:11, :]
    fg_img.wait_recv()
    img_out[...] += fg_rcv[0]
    for cp in sent:
        cp.wait_send()


def body(img_feat, txt_feat, img_weight, txt_weight, logit_scale, logit_bias):
    vm = pl.BlockSpec(memory_space=pltpu.VMEM)
    sm = pl.BlockSpec(memory_space=pltpu.SMEM)
    hbm = pl.BlockSpec(memory_space=pl.ANY)
    V = pltpu.VMEM
    loss, img_grad, txt_grad, w_grad = pl.pallas_call(
        kernel,
        out_shape=(
            jax.ShapeDtypeStruct((8, 128), F32),
            jax.ShapeDtypeStruct((64, FH), F32),
            jax.ShapeDtypeStruct((64, FH), F32),
            jax.ShapeDtypeStruct((11, H), F32),
        ),
        in_specs=[sm, sm, vm, vm, hbm, hbm],
        out_specs=(vm, vm, vm, vm),
        scratch_shapes=[
            V((FEAT, H), BF), V((FEAT, H), BF),
            V((2, 64, H), F32), V((2, R, H), F32), V((2, R, E), F32), V((2, R, 128), F32),
            V((4, 4, R, E), BF), V((2, 8, R, E), BF), V((16 * R, 16 * R), BF), V((4, 64, 512), BF),
            V((3, 4, R, H), BF), V((3, 4, R, H), BF), V((4, R, H), F32), V((3, R, H), BF), V((3, R, H), BF),
            V((3, 4, R, H), BF), V((3, 4, R, H), BF), V((4, R, H), F32), V((3, R, H), BF), V((3, R, H), BF),
            V((8, R, E), BF), V((8, R, E), BF), V((8, R, E), F32),
            V((4, R, E), BF), V((4, R, E), BF), V((4, R, E), BF), V((4, R, E), BF),
            V((2, R, E), BF), V((2, 64, H), BF), V((4, 64, H), BF), V((2, 64, FH), F32), V((2, 64, FH), F32),
            V((528, H), F32), V((16, 16, H), BF), V((16, 16, H), BF), V((8, 16, H), BF), V((8, 16, H), BF),
            V((8, 16, H), BF), V((7, 16, H), BF),
            V((4, 8, 128), F32), V((4, 8, 128), F32), V((2, 8, 128), F32), V((8, 8, 128), F32),
            V((8, 16 * R), F32),
            pltpu.SemaphoreType.DMA((N_SEM,)),
            pltpu.SemaphoreType.DMA((N_SEM,)),
            pltpu.SemaphoreType.DMA((2,)),
        ],
        compiler_params=pltpu.CompilerParams(
            collective_id=0, has_side_effects=True, vmem_limit_bytes=56 * 1024 * 1024
        ),
        name="fused",
    )(logit_scale, logit_bias, img_feat, txt_feat, img_weight, txt_weight)
    return loss[0, 0], img_grad, txt_grad, w_grad


def solution(mesh):
    placed = (P("dp", None), P("dp", None), P(None, "fsdp"), P(None, "fsdp"), P(), P())
    return jax.shard_map(
        body,
        mesh=mesh,
        in_specs=placed,
        out_specs=(P(), P("dp", "fsdp"), P("dp", "fsdp"), P("dp", "fsdp")),
        check_vma=False,
    )
```

time: 1420 us -> 92.1 us (0.06)
  waiting for transfers between devices: 1260 us -> 0 us
  blocking collectives: 92.3 us -> 0 us
  Pallas kernels: 0 us -> 84.1 us
  matrix products: 31.2 us -> 0 us
  between operations: 17.6 us -> 1.93 us
    unnamed x5 -> x0, waiting for transfers between devices: 1010 us -> none
    all_gather x1 -> x0, waiting for transfers between devices: 245 us -> none  [body(): lax.all_gather(key_units, 'dp', axis=0, tiled=True)]
    pallas_call x0 -> x1, Pallas kernels: none -> 84.1 us  [body(): pl.pallas_call(kernel, out_shape=(jax.ShapeDtypeStruct((8, 128), F32), ja...]
    psum x1 -> x0, blocking collectives: 80.1 us -> none  [body(): lax.psum(summed, ('dp', 'fsdp')) * loss_share]
    dot_general x5 -> x0, matrix products: 31.2 us -> none  [the longest x1 13.2 us: sigmoid_terms(): jnp.dot(query_units, block_keys.T, preferred_element_type=jnp.float32)]
  transfers between devices with their start and end apart: 4 -> 0, of which waited for: 3 -> 0; matrix products, arithmetic and copies ran while one was open for 0% -> 0% of each run, Pallas kernels for 0% -> 0%
where the time goes in v1:
time: 92.1 us; the launch traced here: 91.9 us
  Pallas kernels  84.1 us (91%)
  local copies, waits for them, and re-layouts  5.84 us (6%)
  between operations  1.93 us (2%)
    pallas_call x1, Pallas kernels, body(): pl.pallas_call(kernel, out_shape=(jax.ShapeDtypeStruct((8, 128), F32), ja...  84.1 us
    unnamed x3, local copies, waits for them, and re-layouts  4.65 us

profile of v1, /device:TPU:1, one launch (start us, length us, event | category | flops | bytes accessed | tf_op | source)
XLA Modules:
  0.0 91.9 jit_solution(14817504398560239621)
XLA Ops:
  1.9 84.1 %fused.1 = (f32[8,128]{1,0:T(8,128)}, f32[64,704]{1,0:T(8,128)}, f32[64,704]{1,0:T(8,128)}, f32[11,768]{1,0:T(8,128)}) custom-call(f32[1]{0:T(128)S(6)} %copy.13.scale_ref, f32[1]{0:T(128)S(6)} %copy.14.bias_ref, bf16[64,1408]{1,0:T(8,128)(2,1)} %img_feat.1, bf16[64,1408]{1,0:T(8,128)(2,1)} %txt_feat.1, bf16[1408,768]{1,0:T(8,128)(2,1)} %img_w_hbm.1, ...), custom_call_target="tpu_custom_call" | custom-call | tf_op jit(solution)/shard_map/fused/pallas_call | solution.py:396
  86.0 1.2 %slice.3 = f32[1,1]{1,0:T(1,128)} slice(f32[8,128]{1,0:T(8,128)} %get-tuple-element.8), slice={[0:1], [0:1]} | slice | bytes 8 | tf_op jit(solution)/shard_map/slice | solution.py:428
  87.2 1.6 %copy.15 = f32[64,704]{1,0:T(8,128)} copy(f32[64,704]{1,0:T(8,128)} %get-tuple-element.17) | data formatting | bytes 360448
  88.8 1.6 %copy.16 = f32[64,704]{1,0:T(8,128)} copy(f32[64,704]{1,0:T(8,128)} %get-tuple-element.18) | data formatting | bytes 360448
  90.5 1.4 %copy.17 = f32[11,768]{1,0:T(8,128)} copy(f32[11,768]{1,0:T(8,128)} %get-tuple-element.19) | data formatting | bytes 67584

commit v2 on v1

v2 whole, which is shorter than its diff:
```python
import jax
import jax.numpy as jnp
from jax import lax
from jax.experimental import pallas as pl
from jax.experimental.pallas import tpu as pltpu
from jax.sharding import PartitionSpec as P

EPS = 1e-06
MESH = pl.DeviceIdType.MESH
BF = jnp.bfloat16
F32 = jnp.float32
R = 32
E = 1536
H = 768
FEAT = 1408
FH = 704
N_SEM = 160
ORDER = [(2, 2), (2, 1), (2, 3), (1, 2), (3, 2), (1, 1), (1, 3), (3, 1), (3, 3), (2, 0), (0, 2), (1, 0), (3, 0), (0, 1), (0, 3)]


def dot_nt(a, b):
    return lax.dot_general(a, b, (((1,), (1,)), ((), ())), preferred_element_type=F32)


def dot_tn(a, b):
    return lax.dot_general(a, b, (((0,), (0,)), ((), ())), preferred_element_type=F32)


def kernel(
    scale_ref, bias_ref, img_f_hbm, txt_f_hbm, img_w_hbm, txt_w_hbm,
    loss_out, img_out, txt_out, wg_out,
    img_feat, txt_feat, w_img, w_txt, proj, proj_rcv, full, norms,
    txt_all, img_all, slope_s, feat_win,
    a_send, a_rcv, a_own, a2_send, a2_rcv,
    b_send, b_rcv, b_own, b2_send, b2_rcv,
    ci_send, ci_rcv, pi_own, zp_send, zp_rcv, zm_send, zm_rcv,
    pgf, pg64, pg_plane, fi_send, fi_rcv, ft_send, ft_rcv,
    wg, cw_send, cw_rcv, s2, zw_rcv,
    lx, ly, lc, lz, logit_s,
    ssem, rsem, wsem,
):
    dp = lax.axis_index("dp")
    yh = lax.axis_index("fsdp")
    c = lax.rem(dp, 2)
    z = lax.rem(dp // 2, 8)
    yl = lax.rem(dp // 16, 2)
    x = dp // 32
    y = yh * 2 + yl

    def dev(x_, y_, z_, c_):
        return {"dp": ((x_ * 2 + lax.rem(y_, 2)) * 8 + z_) * 2 + c_, "fsdp": y_ // 2}

    def dx(k):
        return dev(lax.rem(x + k, 4), y, z, c)

    def dy(k):
        return dev(x, lax.rem(y + k, 4), z, c)

    def dz(k):
        return dev(x, y, lax.rem(z + k, 8), c)

    other = dev(x, y, z, 1 - c)
    fs_partner = dy(2)

    def dxy(i, j):
        return dev(lax.rem(x + i, 4), lax.rem(y + j, 4), z, c)

    def dyz(k):
        return dev(x, yh * 2 + (1 - yl), lax.rem(z + k, 8), c)

    counter = [0]

    def copy(src, dst, target):
        i = counter[0]
        counter[0] += 1
        cp = pltpu.make_async_remote_copy(
            src_ref=src, dst_ref=dst, send_sem=ssem.at[i], recv_sem=rsem.at[i],
            device_id=target, device_id_type=MESH,
        )
        cp.start()
        sent.append(cp)
        return cp

    sent = []

    loads = [
        pltpu.make_async_copy(img_f_hbm, img_feat, wsem.at[0]),
        pltpu.make_async_copy(img_w_hbm, w_img, wsem.at[1]),
        pltpu.make_async_copy(txt_f_hbm, txt_feat, wsem.at[2]),
        pltpu.make_async_copy(txt_w_hbm, w_txt, wsem.at[3]),
    ]
    for load in loads:
        load.start()

    barrier = pltpu.get_barrier_semaphore()
    partners = [dx(k) for k in (1, 2, 3)] + [dy(k) for k in (1, 2, 3)]
    partners += [dz(k) for k in range(1, 8)] + [other]
    partners += [dxy(i, j) for i in (1, 2, 3) for j in (1, 2, 3)]
    partners += [dyz(k) for k in range(1, 8)]
    for p in partners:
        pl.semaphore_signal(barrier, inc=1, device_id=p, device_id_type=MESH)

    mine = pl.ds(pl.multiple_of(yh * R, R), R)
    theirs = pl.ds(pl.multiple_of((1 - yh) * R, R), R)
    my_cols = pl.ds(pl.multiple_of(yh * H, 128), H)
    their_cols = pl.ds(pl.multiple_of((1 - yh) * H, 128), H)

    def window(x_):
        return pl.ds(pl.multiple_of(256 * x_ + 128 * (x_ // 2), 128), 512)

    loads[0].wait()
    loads[1].wait()
    proj[0] = jnp.dot(img_feat[...], w_img[...], preferred_element_type=F32)
    pl.semaphore_wait(barrier, len(partners))
    swap_img = copy(proj.at[0, theirs], proj_rcv.at[0], fs_partner)
    loads[2].wait()
    loads[3].wait()
    proj[1] = jnp.dot(txt_feat[...], w_txt[...], preferred_element_type=F32)
    swap_txt = copy(proj.at[1, theirs], proj_rcv.at[1], fs_partner)

    fw = []
    for i in (2, 1, 3):
        cols = window(lax.rem(x + i, 4))
        fw.append(copy(txt_feat.at[mine, cols], feat_win.at[4 - i, 0], dx(i)))
        fw.append(copy(txt_feat.at[theirs, cols], feat_win.at[4 - i, 2], dx(i)))
    for i in (2, 1, 3, 0):
        cols = window(lax.rem(x + i, 4))
        for j in (1, 3):
            fw.append(copy(txt_feat.at[mine, cols], feat_win.at[(4 - i) % 4, 4 - j], dxy(i, j)))
    feat_win[0, 0] = txt_feat[mine, window(x)]
    feat_win[0, 2] = txt_feat[theirs, window(x)]

    def embed(m):
        own = proj[m, mine, :]
        got = proj_rcv[m]
        total = jnp.sum(own * own, axis=1, keepdims=True) + jnp.sum(got * got, axis=1, keepdims=True)
        norm = jnp.sqrt(total + EPS)
        norms[m] = jnp.broadcast_to(norm, (R, 128))
        full[m, :, my_cols] = own / norm
        full[m, :, their_cols] = got / norm
        return full[m].astype(BF)

    A = pl.ds(0, H)
    B = pl.ds(H, H)

    zp = {}
    zm = {}
    cf = {}

    swap_img.wait_recv()
    img_all[0, 0] = embed(0)
    for part in (A, B):
        zp[1, part.start] = copy(img_all.at[0, 0, :, part], img_all.at[0, 7, :, part], dz(1))
        zm[1, part.start] = copy(img_all.at[0, 0, :, part], img_all.at[0, 1, :, part], dz(7))
    cf[0] = copy(img_all.at[0, 0], img_all.at[1, 0], other)
    swap_txt.wait_recv()
    txt_all[0, 0] = embed(1)
    ax = {}
    ay = {}
    bx = {}
    by = {}
    for k in (1, 3, 2):
        ax[k] = copy(txt_all.at[0, 0, :, A], txt_all.at[4 - k, 0, :, A], dx(k))
        by[k] = copy(txt_all.at[0, 0, :, B], txt_all.at[0, 4 - k, :, B], dy(k))
    for k in (1, 3, 2):
        ay[0, k] = copy(txt_all.at[0, 0, :, A], txt_all.at[0, 4 - k, :, A], dy(k))
        bx[0, k] = copy(txt_all.at[0, 0, :, B], txt_all.at[4 - k, 0, :, B], dx(k))

    def second(k):
        slot = 4 - k
        ax[k].wait_recv()
        for j in (1, 3, 2):
            ay[slot, j] = copy(txt_all.at[slot, 0, :, A], txt_all.at[slot, 4 - j, :, A], dy(j))
        by[k].wait_recv()
        for j in (1, 3, 2):
            bx[slot, j] = copy(txt_all.at[0, slot, :, B], txt_all.at[4 - j, slot, :, B], dx(j))

    def along_z(step):
        for part in (A, B):
            p = part.start
            zp[step, p].wait_recv()
            if step < 3 or p == 0:
                zp[step + 1, p] = copy(img_all.at[0, 8 - step, :, part], img_all.at[0, 7 - step, :, part], dz(1))
            zm[step, p].wait_recv()
            if step < 3 or p == H:
                zm[step + 1, p] = copy(img_all.at[0, step, :, part], img_all.at[0, step + 1, :, part], dz(7))
        cf[8 - step] = copy(img_all.at[0, 8 - step], img_all.at[1, 8 - step], other)
        cf[step] = copy(img_all.at[0, step], img_all.at[1, step], other)

    along_z(1)
    second(1)
    second(3)
    along_z(2)
    second(2)
    along_z(3)
    zp[4, 0].wait_recv()
    zm[4, H].wait_recv()
    cf[4] = copy(img_all.at[0, 4], img_all.at[1, 4], other)
    for s in range(4):
        for j in (1, 2, 3):
            ay[s, j].wait_recv()
            bx[s, j].wait_recv()
    for s in range(8):
        cf[s].wait_recv()

    scale = scale_ref[...]
    bias = bias_ref[...]
    txt_rows = txt_all[...].reshape(16 * R, E)
    img_rows = img_all[...].reshape(16 * R, E)
    for i in range(2):
        half = slice(i * 8 * R, (i + 1) * 8 * R)
        logit_s[half, :] = dot_nt(img_rows[half], txt_rows)

    def strip(i, acc, diagonal):
        rows = pl.ds(pl.multiple_of(i * R, R), R)
        v = scale * logit_s[rows, :] + bias
        if diagonal:
            ri = lax.broadcasted_iota(jnp.int32, v.shape, 0)
            ci = lax.broadcasted_iota(jnp.int32, v.shape, 1)
            v = jnp.where(ri == ci, -v, v)
        t = jnp.exp(-jnp.abs(v))
        grad = scale * (jnp.where(v >= 0, 1.0, t) / (1.0 + t))
        if diagonal:
            grad = jnp.where(ri == ci, -grad, grad)
        slope_s[rows, :] = grad.astype(BF)
        m = jnp.maximum(v, 0.0)
        prod = t[0:8]
        for j in (8, 16, 24):
            prod = prod + t[j:j + 8] * (1.0 + prod)
        return acc + jnp.log1p(prod) + ((m[0:8] + m[8:16]) + (m[16:24] + m[24:32]))

    acc = strip(0, jnp.zeros((8, 16 * R), F32), True)
    acc = lax.fori_loop(1, 16, lambda i, a: strip(i, a, False), acc, unroll=3)

    sa = {}
    sb = {}
    for k in (1, 3, 2, 0):
        g = dot_tn(slope_s[:, k * 128:(k + 1) * 128], img_rows)
        ga = g[:, :H].reshape(4, R, H)
        gb = g[:, H:].reshape(4, R, H)
        if k:
            a_send[k - 1] = ga.astype(BF)
            sa[k] = copy(a_send.at[k - 1], a_rcv.at[3 - k], dx(k))
        else:
            a_own[...] = ga
        b_own[k] = gb[0]
        b_send[:, k] = gb[1:].astype(BF)
        for j in (1, 3, 2):
            sb[j, k] = copy(b_send.at[j - 1, k], b_rcv.at[3 - j, k], dy(j))

    ci_send[...] = jnp.dot(
        slope_s[8 * R:, :], txt_rows, preferred_element_type=F32
    ).astype(BF).reshape(8, R, E)
    ci_copy = copy(ci_send, ci_rcv, other)
    pi_own[...] = jnp.dot(slope_s[:8 * R, :], txt_rows, preferred_element_type=F32).reshape(8, R, E)

    part = jnp.sum(acc)
    lx[0] = jnp.full((8, 128), part, F32)
    lxc = [copy(lx.at[0], lx.at[4 - k], dx(k)) for k in (1, 2, 3)]

    ci_copy.wait_recv()
    pi_own[...] += ci_rcv[...].astype(F32)

    zp_send[0] = pi_own[4].astype(BF)
    rzp = [copy(zp_send.at[0, :, A], zp_rcv.at[0, :, A], dz(1))]
    rzm = [copy(zp_send.at[0, :, B], zm_rcv.at[0, :, B], dz(7))]

    def ring(step):
        rzp[step - 1].wait_recv()
        rzm[step - 1].wait_recv()
        if step == 1:
            zp_send[1, :, A] = (pi_own[3, :, A] + zp_rcv[0, :, A].astype(F32)).astype(BF)
            zp_send[1, :, B] = pi_own[3, :, B].astype(BF)
            zm_send[1, :, B] = (pi_own[5, :, B] + zm_rcv[0, :, B].astype(F32)).astype(BF)
            zm_send[1, :, A] = pi_own[5, :, A].astype(BF)
        else:
            zp_send[step] = (pi_own[4 - step] + zp_rcv[step - 1].astype(F32)).astype(BF)
            zm_send[step] = (pi_own[4 + step] + zm_rcv[step - 1].astype(F32)).astype(BF)
        rzp.append(copy(zp_send.at[step], zp_rcv.at[step], dz(1)))
        rzm.append(copy(zm_send.at[step], zm_rcv.at[step], dz(7)))

    ring(1)
    ring(2)

    for k in (1, 2, 3):
        sa[k].wait_recv()
    ga = a_own[...] + a_rcv[0].astype(F32) + a_rcv[1].astype(F32) + a_rcv[2].astype(F32)
    a2_send[...] = ga[1:].astype(BF)
    a2 = [copy(a2_send.at[k - 1], a2_rcv.at[3 - k], dy(k)) for k in (1, 2, 3)]
    for cp in sb.values():
        cp.wait_recv()
    gb = b_own[...] + b_rcv[0].astype(F32) + b_rcv[1].astype(F32) + b_rcv[2].astype(F32)
    b2_send[...] = gb[1:].astype(BF)
    b2 = [copy(b2_send.at[k - 1], b2_rcv.at[3 - k], dx(k)) for k in (1, 2, 3)]
    ga0 = ga[0]
    gb0 = gb[0]

    for cp in lxc:
        cp.wait_recv()
    ly[0] = (lx[0] + lx[2]) + (lx[1] + lx[3])
    lyc = [copy(ly.at[0], ly.at[4 - k], dy(k)) for k in (1, 2, 3)]

    ring(3)

    for cp in a2:
        cp.wait_recv()
    for cp in b2:
        cp.wait_recv()
    ga0 = ga0 + a2_rcv[0].astype(F32) + a2_rcv[1].astype(F32) + a2_rcv[2].astype(F32)
    gb0 = gb0 + b2_rcv[0].astype(F32) + b2_rcv[1].astype(F32) + b2_rcv[2].astype(F32)

    def back(m, ga, gb):
        ua = full[m, :, A]
        ub = full[m, :, B]
        inner = jnp.sum(ua * ga, axis=1, keepdims=True) + jnp.sum(ub * gb, axis=1, keepdims=True)
        norm = norms[m, :, 0:1]
        pgf[m, :, A] = ((ga - ua * inner) / norm).astype(BF)
        pgf[m, :, B] = ((gb - ub * inner) / norm).astype(BF)

    def share(m):
        cp = copy(pgf.at[m, :, their_cols], pg64.at[m, mine], fs_partner)
        pg64[m, mine, :] = pgf[m, :, my_cols]
        return cp

    back(1, ga0, gb0)

    def quarter(y_):
        return pl.ds(pl.multiple_of(384 * y_, 128), 384)

    pp = [
        copy(
            pgf.at[1, :, quarter(lax.rem(y + j, 4))],
            pg_plane.at[(4 - i) % 4, (4 - j) % 4], dxy(i, j),
        )
        for i, j in ORDER
    ]
    pg_plane[0, 0] = pgf[1, :, quarter(y)]
    pg_txt = share(1)

    rzp[3].wait_recv()
    rzm[3].wait_recv()
    gi = pi_own[0] + zp_rcv[3].astype(F32) + zm_rcv[3].astype(F32)
    back(0, gi[:, :H], gi[:, H:])
    pg_img = share(0)

    my_feat = pl.ds(pl.multiple_of(yh * FH, 16), FH)
    their_feat = pl.ds(pl.multiple_of((1 - yh) * FH, 16), FH)

    def feature_terms(m, w, out, into):
        out[...] = dot_nt(pg64[m], w[their_feat, :]).astype(out.dtype)
        return copy(out, into, fs_partner)

    for cp in lyc:
        cp.wait_recv()
    lc[0] = (ly[0] + ly[2]) + (ly[1] + ly[3])
    lcc = copy(lc.at[0], lc.at[1], other)
    for cp in fw:
        cp.wait_recv()
    for cp in pp:
        cp.wait_recv()
    wg[0:512, :] = dot_tn(feat_win[...].reshape(16 * R, 512), pg_plane[...].reshape(16 * R, 384))
    wg[512:528, :] = jnp.zeros((16, 384), F32)
    start = 352 * x - (256 * x + 128 * (x // 2))

    def rows16(k, core):
        first = start + 22 * k + 11 * core
        low = first // 8
        block = wg[pl.ds(pl.multiple_of(low * 8, 8), 24), :]
        return pltpu.roll(block, 24 - (first - low * 8), 0)[:16]

    def cut(k, carry):
        cw_send[k] = rows16(k, 1 - c).astype(BF)
        return carry

    lax.fori_loop(0, 16, cut, 0, unroll=4)
    cw = copy(cw_send, cw_rcv, other)

    pg_txt.wait_recv()
    fg_txt = feature_terms(1, w_txt, ft_send, ft_rcv)
    pg_img.wait_recv()
    fg_img = feature_terms(0, w_img, fi_send, fi_rcv)
    lcc.wait_recv()
    lz[0] = lc[0] + lc[1]
    lzc = [copy(lz.at[0], lz.at[8 - k], dz(k)) for k in range(1, 8)]

    cw.wait_recv()

    def add_core(k, carry):
        s2[k] = (rows16(k, c) + cw_rcv[k].astype(F32)).astype(BF)
        return carry

    lax.fori_loop(0, 16, add_core, 0, unroll=4)
    zw = []
    for k in (4, 3, 5, 2, 6, 1, 7, 0):
        zz = lax.rem(z + k, 8)
        zw.append(copy(s2.at[(1 - yl) * 8 + zz], zw_rcv.at[1, (8 - k) % 8], dyz(k)))
        if k:
            zw.append(copy(s2.at[yl * 8 + zz], zw_rcv.at[0, 8 - k], dz(k)))

    txt_out[...] = dot_nt(pg64[1], w_txt[my_feat, :])
    img_out[...] = dot_nt(pg64[0], w_img[my_feat, :])

    near = rows16(yl * 8 + z, c) + cw_rcv[yl * 8 + z].astype(F32)
    fg_txt.wait_recv()
    txt_out[...] += ft_rcv[...].astype(F32)
    for cp in lzc:
        cp.wait_recv()
    total = ((lz[0] + lz[4]) + (lz[2] + lz[6])) + ((lz[1] + lz[5]) + (lz[3] + lz[7]))
    loss_out[0] = jnp.max(total) / 8192.0
    for cp in zw:
        cp.wait_recv()
    far = zw_rcv[1, 0].astype(F32)
    for k in range(1, 8):
        near = near + zw_rcv[0, k].astype(F32)
        far = far + zw_rcv[1, k].astype(F32)
    wg_out[:, pl.ds(pl.multiple_of(384 * yl, 128), 384)] = near[:11, :]
    wg_out[:, pl.ds(pl.multiple_of(384 * (1 - yl), 128), 384)] = far[:11, :]
    fg_img.wait_recv()
    img_out[...] += fi_rcv[...]
    for cp in sent:
        cp.wait_send()


def hand_out(*refs):
    refs[4][0] = refs[0][0]
    for i in (1, 2, 3):
        refs[4 + i][...] = refs[i][...]


def body(img_feat, txt_feat, img_weight, txt_weight, logit_scale, logit_bias):
    vm = pl.BlockSpec(memory_space=pltpu.VMEM)
    sm = pl.BlockSpec(memory_space=pltpu.SMEM)
    hbm = pl.BlockSpec(memory_space=pltpu.HBM)
    V = pltpu.VMEM
    results = pl.pallas_call(
        kernel,
        out_shape=(
            jax.ShapeDtypeStruct((1,), F32),
            jax.ShapeDtypeStruct((64, FH), F32),
            jax.ShapeDtypeStruct((64, FH), F32),
            jax.ShapeDtypeStruct((11, H), F32),
        ),
        in_specs=[vm, vm, hbm, hbm, hbm, hbm],
        out_specs=(sm, vm, vm, vm),
        scratch_shapes=[
            V((64, FEAT), BF), V((64, FEAT), BF), V((FEAT, H), BF), V((FEAT, H), BF),
            V((2, 64, H), F32), V((2, R, H), F32), V((2, R, E), F32), V((2, R, 128), F32),
            V((4, 4, R, E), BF), V((2, 8, R, E), BF), V((16 * R, 16 * R), BF), V((4, 4, R, 512), BF),
            V((3, 4, R, H), BF), V((3, 4, R, H), BF), V((4, R, H), F32), V((3, R, H), BF), V((3, R, H), BF),
            V((3, 4, R, H), BF), V((3, 4, R, H), BF), V((4, R, H), F32), V((3, R, H), BF), V((3, R, H), BF),
            V((8, R, E), BF), V((8, R, E), BF), V((8, R, E), F32),
            V((4, R, E), BF), V((4, R, E), BF), V((4, R, E), BF), V((4, R, E), BF),
            V((2, R, E), BF), V((2, 64, H), BF), V((4, 4, R, 384), BF), V((64, FH), F32), V((64, FH), F32), V((64, FH), BF), V((64, FH), BF),
            V((528, 384), F32), V((16, 16, 384), BF), V((16, 16, 384), BF), V((16, 16, 384), BF), V((2, 8, 16, 384), BF),
            V((4, 8, 128), F32), V((4, 8, 128), F32), V((2, 8, 128), F32), V((8, 8, 128), F32),
            V((16 * R, 16 * R), F32),
            pltpu.SemaphoreType.DMA((N_SEM,)),
            pltpu.SemaphoreType.DMA((N_SEM,)),
            pltpu.SemaphoreType.DMA((4,)),
        ],
        compiler_params=pltpu.CompilerParams(
            collective_id=0, has_side_effects=True, vmem_limit_bytes=56 * 1024 * 1024
        ),
        name="fused",
    )(logit_scale.reshape(1, 1), logit_bias.reshape(1, 1), img_feat, txt_feat, img_weight, txt_weight)
    loss, img_grad, txt_grad, w_grad = pl.pallas_call(
        hand_out,
        out_shape=tuple(jax.ShapeDtypeStruct(r.shape, r.dtype) for r in results),
        in_specs=[sm, vm, vm, vm],
        out_specs=(sm, vm, vm, vm),
        name="hand_out",
    )(*results)
    return loss.reshape(()), img_grad, txt_grad, w_grad


def solution(mesh):
    placed = (P("dp", None), P("dp", None), P(None, "fsdp"), P(None, "fsdp"), P(), P())
    return jax.shard_map(
        body,
        mesh=mesh,
        in_specs=placed,
        out_specs=(P(), P("dp", "fsdp"), P("dp", "fsdp"), P("dp", "fsdp")),
        check_vma=False,
    )
```

time: 92.1 us -> 78.8 us (0.86)
  Pallas kernels: 84.1 us -> 76.8 us
  local copies, waits for them, and re-layouts: 5.84 us -> 0 us
    pallas_call x1 -> x2, Pallas kernels: 84.1 us -> 76.8 us  [the longest x1 74.3 us: body(): pl.pallas_call(kernel, out_shape=(jax.ShapeDtypeStruct((1,), F32), jax.Sh...]
    unnamed x3 -> x0, local copies, waits for them, and re-layouts: 4.65 us -> none
    slice x1 -> x0, local copies, waits for them, and re-layouts: 1.19 us -> none  [body(): return (loss[0, 0], img_grad, txt_grad, w_grad)]
where the time goes in v2:
time: 78.8 us; the launch traced here: 78.7 us
  Pallas kernels  76.8 us (97%)
  between operations  1.93 us (2%)
    pallas_call x1, Pallas kernels, body(): pl.pallas_call(kernel, out_shape=(jax.ShapeDtypeStruct((1,), F32), jax.Sh...  74.3 us
    pallas_call x1, Pallas kernels, body(): pl.pallas_call(hand_out, out_shape=tuple((jax.ShapeDtypeStruct(r.shape, r...  2.48 us

profile of v2, /device:TPU:1, one launch (start us, length us, event | category | flops | bytes accessed | tf_op | source)
XLA Modules:
  0.0 78.7 jit_solution(18019681733968179536)
XLA Ops:
  1.9 74.3 %fused.1 = (f32[1]{0:T(128)}, f32[64,704]{1,0:T(8,128)}, f32[64,704]{1,0:T(8,128)}, f32[11,768]{1,0:T(8,128)}) custom-call(f32[1,1]{1,0:T(1,128)} %bitcast.3.scale_ref, f32[1,1]{1,0:T(1,128)} %bitcast.4.bias_ref, bf16[64,1408]{1,0:T(8,128)(2,1)} %img_f_hbm.1, bf16[64,1408]{1,0:T(8,128)(2,1)} %txt_f_hbm.1, bf16[1408,768]{1,0:T(8,128)(2,1)} %img_w_hbm.1, ...), custom_call_target="tpu_custom_call" | custom-call | tf_op jit(solution)/shard_map/fused/pallas_call | solution.py:435
  76.2 2.5 %hand_out.1 = (f32[1]{0:T(128)}, f32[64,704]{1,0:T(8,128)}, f32[64,704]{1,0:T(8,128)}, f32[11,768]{1,0:T(8,128)}) custom-call(f32[1]{0:T(128)} %get-tuple-element.12.refs_0_, f32[64,704]{1,0:T(8,128)} %get-tuple-element.13.refs_1_, f32[64,704]{1,0:T(8,128)} %get-tuple-element.14.refs_2_, f32[11,768]{1,0:T(8,128)} %get-tuple-element.15.refs_3_), custom_call_target="tpu_custom_call" | custom-call | tf_op jit(solution)/shard_map/hand_out/pallas_call | solution.py:466

commit v3 on v2

--- a/solution.py
+++ b/solution.py
@@ -14,7 +14,7 @@
 H = 768
 FEAT = 1408
 FH = 704
-N_SEM = 160
+N_SEM = 192
 ORDER = [(2, 2), (2, 1), (2, 3), (1, 2), (3, 2), (1, 1), (1, 3), (3, 1), (3, 3), (2, 0), (0, 2), (1, 0), (3, 0), (0, 1), (0, 3)]
 
 
@@ -30,7 +30,7 @@
     scale_ref, bias_ref, img_f_hbm, txt_f_hbm, img_w_hbm, txt_w_hbm,
     loss_out, img_out, txt_out, wg_out,
     img_feat, txt_feat, w_img, w_txt, proj, proj_rcv, full, norms,
-    txt_all, img_all, slope_s, feat_win,
+    txt_all, img_all, slope_s, feat_win, feat_y,
     a_send, a_rcv, a_own, a2_send, a2_rcv,
     b_send, b_rcv, b_own, b2_send, b2_rcv,
     ci_send, ci_rcv, pi_own, zp_send, zp_rcv, zm_send, zm_rcv,
@@ -94,9 +94,7 @@
 
     barrier = pltpu.get_barrier_semaphore()
     partners = [dx(k) for k in (1, 2, 3)] + [dy(k) for k in (1, 2, 3)]
-    partners += [dz(k) for k in range(1, 8)] + [other]
-    partners += [dxy(i, j) for i in (1, 2, 3) for j in (1, 2, 3)]
-    partners += [dyz(k) for k in range(1, 8)]
+    partners += [dz(1), dz(7), other]
     for p in partners:
         pl.semaphore_signal(barrier, inc=1, device_id=p, device_id_type=MESH)
 
@@ -119,16 +117,20 @@
     swap_txt = copy(proj.at[1, theirs], proj_rcv.at[1], fs_partner)
 
     fw = []
-    for i in (2, 1, 3):
+    fy = [copy(txt_feat.at[mine], feat_y.at[1], dy(1)), copy(txt_feat.at[mine], feat_y.at[0], dy(3))]
+
+    def features(own, i):
         cols = window(lax.rem(x + i, 4))
-        fw.append(copy(txt_feat.at[mine, cols], feat_win.at[4 - i, 0], dx(i)))
-        fw.append(copy(txt_feat.at[theirs, cols], feat_win.at[4 - i, 2], dx(i)))
+        slot = (4 - i) % 4
+        sources = (txt_feat.at[mine, cols], feat_y.at[0, :, cols], txt_feat.at[theirs, cols], feat_y.at[1, :, cols])
+        for j in (0, 2) if own else (1, 3):
+            if i:
+                fw.append(copy(sources[j], feat_win.at[slot, j], dx(i)))
+            else:
+                feat_win[0, j] = sources[j][...]
+
     for i in (2, 1, 3, 0):
-        cols = window(lax.rem(x + i, 4))
-        for j in (1, 3):
-            fw.append(copy(txt_feat.at[mine, cols], feat_win.at[(4 - i) % 4, 4 - j], dxy(i, j)))
-    feat_win[0, 0] = txt_feat[mine, window(x)]
-    feat_win[0, 2] = txt_feat[theirs, window(x)]
+        features(True, i)
 
     def embed(m):
         own = proj[m, mine, :]
@@ -149,9 +151,10 @@
 
     swap_img.wait_recv()
     img_all[0, 0] = embed(0)
-    for part in (A, B):
-        zp[1, part.start] = copy(img_all.at[0, 0, :, part], img_all.at[0, 7, :, part], dz(1))
-        zm[1, part.start] = copy(img_all.at[0, 0, :, part], img_all.at[0, 1, :, part], dz(7))
+    parts = [pl.ds(384 * q, 384) for q in range(4)]
+    for q, part in enumerate(parts):
+        zp[1, q] = copy(img_all.at[0, 0, :, part], img_all.at[0, 7, :, part], dz(1))
+        zm[1, q] = copy(img_all.at[0, 0, :, part], img_all.at[0, 1, :, part], dz(7))
     cf[0] = copy(img_all.at[0, 0], img_all.at[1, 0], other)
     swap_txt.wait_recv()
     txt_all[0, 0] = embed(1)
@@ -176,14 +179,13 @@
             bx[slot, j] = copy(txt_all.at[0, slot, :, B], txt_all.at[4 - j, slot, :, B], dx(j))
 
     def along_z(step):
-        for part in (A, B):
-            p = part.start
-            zp[step, p].wait_recv()
-            if step < 3 or p == 0:
-                zp[step + 1, p] = copy(img_all.at[0, 8 - step, :, part], img_all.at[0, 7 - step, :, part], dz(1))
-            zm[step, p].wait_recv()
-            if step < 3 or p == H:
-                zm[step + 1, p] = copy(img_all.at[0, step, :, part], img_all.at[0, step + 1, :, part], dz(7))
+        for q, part in enumerate(parts):
+            zp[step, q].wait_recv()
+            if step < 3 or q < 2:
+                zp[step + 1, q] = copy(img_all.at[0, 8 - step, :, part], img_all.at[0, 7 - step, :, part], dz(1))
+            zm[step, q].wait_recv()
+            if step < 3 or q >= 2:
+                zm[step + 1, q] = copy(img_all.at[0, step, :, part], img_all.at[0, step + 1, :, part], dz(7))
         cf[8 - step] = copy(img_all.at[0, 8 - step], img_all.at[1, 8 - step], other)
         cf[step] = copy(img_all.at[0, step], img_all.at[1, step], other)
 
@@ -193,24 +195,23 @@
     along_z(2)
     second(2)
     along_z(3)
-    zp[4, 0].wait_recv()
-    zm[4, H].wait_recv()
+    for q in (0, 1):
+        zp[4, q].wait_recv()
+        zm[4, q + 2].wait_recv()
     cf[4] = copy(img_all.at[0, 4], img_all.at[1, 4], other)
     for s in range(4):
         for j in (1, 2, 3):
             ay[s, j].wait_recv()
             bx[s, j].wait_recv()
-    for s in range(8):
-        cf[s].wait_recv()
+
+    for cp in fy:
+        cp.wait_recv()
+    for i in (2, 1, 3, 0):
+        features(False, i)
 
     scale = scale_ref[...]
     bias = bias_ref[...]
     txt_rows = txt_all[...].reshape(16 * R, E)
-    img_rows = img_all[...].reshape(16 * R, E)
-    for i in range(2):
-        half = slice(i * 8 * R, (i + 1) * 8 * R)
-        logit_s[half, :] = dot_nt(img_rows[half], txt_rows)
-
     def strip(i, acc, diagonal):
         rows = pl.ds(pl.multiple_of(i * R, R), R)
         v = scale * logit_s[rows, :] + bias
@@ -229,18 +230,25 @@
             prod = prod + t[j:j + 8] * (1.0 + prod)
         return acc + jnp.log1p(prod) + ((m[0:8] + m[8:16]) + (m[16:24] + m[24:32]))
 
+    logit_s[0:8 * R, :] = dot_nt(img_all[0].reshape(8 * R, E), txt_rows)
     acc = strip(0, jnp.zeros((8, 16 * R), F32), True)
-    acc = lax.fori_loop(1, 16, lambda i, a: strip(i, a, False), acc, unroll=3)
+    acc = lax.fori_loop(1, 8, lambda i, a: strip(i, a, False), acc, unroll=True)
+    for s in range(8):
+        cf[s].wait_recv()
+    logit_s[8 * R:, :] = dot_nt(img_all[1].reshape(8 * R, E), txt_rows)
+    acc = lax.fori_loop(8, 16, lambda i, a: strip(i, a, False), acc, unroll=4)
+    img_rows = img_all[...].reshape(16 * R, E)
 
     sa = {}
     sb = {}
-    for k in (1, 3, 2, 0):
+
+    def text_grads(k):
         g = dot_tn(slope_s[:, k * 128:(k + 1) * 128], img_rows)
         ga = g[:, :H].reshape(4, R, H)
         gb = g[:, H:].reshape(4, R, H)
         if k:
             a_send[k - 1] = ga.astype(BF)
-            sa[k] = copy(a_send.at[k - 1], a_rcv.at[3 - k], dx(k))
+            sa[k] = copy(a_send.at[k - 1, 1:], a_rcv.at[3 - k, 1:], dx(k))
         else:
             a_own[...] = ga
         b_own[k] = gb[0]
@@ -248,10 +256,17 @@
         for j in (1, 3, 2):
             sb[j, k] = copy(b_send.at[j - 1, k], b_rcv.at[3 - j, k], dy(j))
 
+    text_grads(1)
+    text_grads(3)
     ci_send[...] = jnp.dot(
         slope_s[8 * R:, :], txt_rows, preferred_element_type=F32
     ).astype(BF).reshape(8, R, E)
     ci_copy = copy(ci_send, ci_rcv, other)
+    text_grads(2)
+    text_grads(0)
+    for k in (1, 3, 2):
+        sa[k, 0] = copy(a_send.at[k - 1, 0], a_rcv.at[3 - k, 0], dx(k))
+
     pi_own[...] = jnp.dot(slope_s[:8 * R, :], txt_rows, preferred_element_type=F32).reshape(8, R, E)
 
     part = jnp.sum(acc)
@@ -261,53 +276,66 @@
     ci_copy.wait_recv()
     pi_own[...] += ci_rcv[...].astype(F32)
 
-    zp_send[0] = pi_own[4].astype(BF)
-    rzp = [copy(zp_send.at[0, :, A], zp_rcv.at[0, :, A], dz(1))]
-    rzm = [copy(zp_send.at[0, :, B], zm_rcv.at[0, :, B], dz(7))]
+    rzp = {}
+    rzm = {}
+
+    def send_p(step, q, value):
+        zp_send[step, :, parts[q]] = value.astype(BF)
+        rzp[step, q] = copy(zp_send.at[step, :, parts[q]], zp_rcv.at[step, :, parts[q]], dz(1))
+
+    def send_m(step, q, value):
+        zm_send[step, :, parts[q]] = value.astype(BF)
+        rzm[step, q] = copy(zm_send.at[step, :, parts[q]], zm_rcv.at[step, :, parts[q]], dz(7))
+
+    for q in (0, 1):
+        send_p(0, q, pi_own[4, :, parts[q]])
+        send_m(0, q + 2, pi_own[4, :, parts[q + 2]])
+    for q in (0, 1):
+        send_p(1, q + 2, pi_own[3, :, parts[q + 2]])
+        send_m(1, q, pi_own[5, :, parts[q]])
 
     def ring(step):
-        rzp[step - 1].wait_recv()
-        rzm[step - 1].wait_recv()
-        if step == 1:
-            zp_send[1, :, A] = (pi_own[3, :, A] + zp_rcv[0, :, A].astype(F32)).astype(BF)
-            zp_send[1, :, B] = pi_own[3, :, B].astype(BF)
-            zm_send[1, :, B] = (pi_own[5, :, B] + zm_rcv[0, :, B].astype(F32)).astype(BF)
-            zm_send[1, :, A] = pi_own[5, :, A].astype(BF)
-        else:
-            zp_send[step] = (pi_own[4 - step] + zp_rcv[step - 1].astype(F32)).astype(BF)
-            zm_send[step] = (pi_own[4 + step] + zm_rcv[step - 1].astype(F32)).astype(BF)
-        rzp.append(copy(zp_send.at[step], zp_rcv.at[step], dz(1)))
-        rzm.append(copy(zm_send.at[step], zm_rcv.at[step], dz(7)))
+        for q in (0, 1) if step == 1 else (2, 3, 0, 1):
+            r = (q + 2) % 4
+            rzp[step - 1, q].wait_recv()
+            send_p(step, q, pi_own[4 - step, :, parts[q]] + zp_rcv[step - 1, :, parts[q]].astype(F32))
+            rzm[step - 1, r].wait_recv()
+            send_m(step, r, pi_own[4 + step, :, parts[r]] + zm_rcv[step - 1, :, parts[r]].astype(F32))
 
     ring(1)
-    ring(2)
+
+    def summed(own, got):
+        return own + got[0].astype(F32) + got[1].astype(F32) + got[2].astype(F32)
 
     for k in (1, 2, 3):
         sa[k].wait_recv()
-    ga = a_own[...] + a_rcv[0].astype(F32) + a_rcv[1].astype(F32) + a_rcv[2].astype(F32)
-    a2_send[...] = ga[1:].astype(BF)
+    a2_send[...] = summed(a_own[1:], [a_rcv[k, 1:] for k in range(3)]).astype(BF)
     a2 = [copy(a2_send.at[k - 1], a2_rcv.at[3 - k], dy(k)) for k in (1, 2, 3)]
-    for cp in sb.values():
-        cp.wait_recv()
-    gb = b_own[...] + b_rcv[0].astype(F32) + b_rcv[1].astype(F32) + b_rcv[2].astype(F32)
-    b2_send[...] = gb[1:].astype(BF)
+    for k in (1, 2, 3):
+        for j in (1, 2, 3):
+            sb[j, k].wait_recv()
+    b2_send[...] = summed(b_own[1:], [b_rcv[k, 1:] for k in range(3)]).astype(BF)
     b2 = [copy(b2_send.at[k - 1], b2_rcv.at[3 - k], dx(k)) for k in (1, 2, 3)]
-    ga0 = ga[0]
-    gb0 = gb[0]
+    for k in (1, 2, 3):
+        sa[k, 0].wait_recv()
+        sb[k, 0].wait_recv()
+    ga0 = summed(a_own[0], [a_rcv[k, 0] for k in range(3)])
+    gb0 = summed(b_own[0], [b_rcv[k, 0] for k in range(3)])
 
     for cp in lxc:
         cp.wait_recv()
     ly[0] = (lx[0] + lx[2]) + (lx[1] + lx[3])
     lyc = [copy(ly.at[0], ly.at[4 - k], dy(k)) for k in (1, 2, 3)]
 
+    ring(2)
     ring(3)
 
     for cp in a2:
         cp.wait_recv()
     for cp in b2:
         cp.wait_recv()
-    ga0 = ga0 + a2_rcv[0].astype(F32) + a2_rcv[1].astype(F32) + a2_rcv[2].astype(F32)
-    gb0 = gb0 + b2_rcv[0].astype(F32) + b2_rcv[1].astype(F32) + b2_rcv[2].astype(F32)
+    ga0 = summed(ga0, a2_rcv)
+    gb0 = summed(gb0, b2_rcv)
 
     def back(m, ga, gb):
         ua = full[m, :, A]
@@ -323,6 +351,7 @@
         return cp
 
     back(1, ga0, gb0)
+    pg_txt = share(1)
 
     def quarter(y_):
         return pl.ds(pl.multiple_of(384 * y_, 128), 384)
@@ -335,10 +364,10 @@
         for i, j in ORDER
     ]
     pg_plane[0, 0] = pgf[1, :, quarter(y)]
-    pg_txt = share(1)
-
-    rzp[3].wait_recv()
-    rzm[3].wait_recv()
+
+    for q in range(4):
+        rzp[3, q].wait_recv()
+        rzm[3, q].wait_recv()
     gi = pi_own[0] + zp_rcv[3].astype(F32) + zm_rcv[3].astype(F32)
     back(0, gi[:, :H], gi[:, H:])
     pg_img = share(0)
@@ -350,6 +379,8 @@
         out[...] = dot_nt(pg64[m], w[their_feat, :]).astype(out.dtype)
         return copy(out, into, fs_partner)
 
+    pg_txt.wait_recv()
+    fg_txt = feature_terms(1, w_txt, ft_send, ft_rcv)
     for cp in lyc:
         cp.wait_recv()
     lc[0] = (ly[0] + ly[2]) + (ly[1] + ly[3])
@@ -375,8 +406,6 @@
     lax.fori_loop(0, 16, cut, 0, unroll=4)
     cw = copy(cw_send, cw_rcv, other)
 
-    pg_txt.wait_recv()
-    fg_txt = feature_terms(1, w_txt, ft_send, ft_rcv)
     pg_img.wait_recv()
     fg_img = feature_terms(0, w_img, fi_send, fi_rcv)
     lcc.wait_recv()
@@ -445,7 +474,7 @@
         scratch_shapes=[
             V((64, FEAT), BF), V((64, FEAT), BF), V((FEAT, H), BF), V((FEAT, H), BF),
             V((2, 64, H), F32), V((2, R, H), F32), V((2, R, E), F32), V((2, R, 128), F32),
-            V((4, 4, R, E), BF), V((2, 8, R, E), BF), V((16 * R, 16 * R), BF), V((4, 4, R, 512), BF),
+            V((4, 4, R, E), BF), V((2, 8, R, E), BF), V((16 * R, 16 * R), BF), V((4, 4, R, 512), BF), V((2, R, FEAT), BF),
             V((3, 4, R, H), BF), V((3, 4, R, H), BF), V((4, R, H), F32), V((3, R, H), BF), V((3, R, H), BF),
             V((3, 4, R, H), BF), V((3, 4, R, H), BF), V((4, R, H), F32), V((3, R, H), BF), V((3, R, H), BF),
             V((8, R, E), BF), V((8, R, E), BF), V((8, R, E), F32),

time: 78.8 us -> 74.6 us (0.947)
  Pallas kernels: 76.8 us -> 72.6 us
    pallas_call x1, Pallas kernels: 74.3 us -> 70.1 us  [body(): pl.pallas_call(kernel, out_shape=(jax.ShapeDtypeStruct((1,), F32), jax.Sh...]
where the time goes in v3:
time: 74.6 us; the launch traced here: 74.5 us
  Pallas kernels  72.6 us (97%)
  between operations  1.93 us (3%)
    pallas_call x1, Pallas kernels, body(): pl.pallas_call(kernel, out_shape=(jax.ShapeDtypeStruct((1,), F32), jax.Sh...  70.1 us
    pallas_call x1, Pallas kernels, body(): pl.pallas_call(hand_out, out_shape=tuple((jax.ShapeDtypeStruct(r.shape, r...  2.48 us

profile of v3, /device:TPU:1, one launch (start us, length us, event | category | flops | bytes accessed | tf_op | source)
XLA Modules:
  0.0 74.5 jit_solution(13414379528799550690)
XLA Ops:
  1.9 70.1 %fused.1 = (f32[1]{0:T(128)}, f32[64,704]{1,0:T(8,128)}, f32[64,704]{1,0:T(8,128)}, f32[11,768]{1,0:T(8,128)}) custom-call(f32[1,1]{1,0:T(1,128)} %bitcast.3.scale_ref, f32[1,1]{1,0:T(1,128)} %bitcast.4.bias_ref, bf16[64,1408]{1,0:T(8,128)(2,1)} %img_f_hbm.1, bf16[64,1408]{1,0:T(8,128)(2,1)} %txt_f_hbm.1, bf16[1408,768]{1,0:T(8,128)(2,1)} %img_w_hbm.1, ...), custom_call_target="tpu_custom_call" | custom-call | tf_op jit(solution)/shard_map/fused/pallas_call | solution.py:464
  72.0 2.5 %hand_out.1 = (f32[1]{0:T(128)}, f32[64,704]{1,0:T(8,128)}, f32[64,704]{1,0:T(8,128)}, f32[11,768]{1,0:T(8,128)}) custom-call(f32[1]{0:T(128)} %get-tuple-element.12.refs_0_, f32[64,704]{1,0:T(8,128)} %get-tuple-element.13.refs_1_, f32[64,704]{1,0:T(8,128)} %get-tuple-element.14.refs_2_, f32[11,768]{1,0:T(8,128)} %get-tuple-element.15.refs_3_), custom_call_target="tpu_custom_call" | custom-call | tf_op jit(solution)/shard_map/hand_out/pallas_call | solution.py:495

commit v4 on v3

--- a/solution.py
+++ b/solution.py
@@ -14,7 +14,7 @@
 H = 768
 FEAT = 1408
 FH = 704
-N_SEM = 192
+N_SEM = 240
 ORDER = [(2, 2), (2, 1), (2, 3), (1, 2), (3, 2), (1, 1), (1, 3), (3, 1), (3, 3), (2, 0), (0, 2), (1, 0), (3, 0), (0, 1), (0, 3)]
 
 
@@ -31,7 +31,7 @@
     loss_out, img_out, txt_out, wg_out,
     img_feat, txt_feat, w_img, w_txt, proj, proj_rcv, full, norms,
     txt_all, img_all, slope_s, feat_win, feat_y,
-    a_send, a_rcv, a_own, a2_send, a2_rcv,
+    a_mid, b_mid, a_send, a_rcv, a_own, a2_send, a2_rcv,
     b_send, b_rcv, b_own, b2_send, b2_rcv,
     ci_send, ci_rcv, pi_own, zp_send, zp_rcv, zm_send, zm_rcv,
     pgf, pg64, pg_plane, fi_send, fi_rcv, ft_send, ft_rcv,
@@ -239,6 +239,8 @@
     acc = lax.fori_loop(8, 16, lambda i, a: strip(i, a, False), acc, unroll=4)
     img_rows = img_all[...].reshape(16 * R, E)
 
+    left = pl.ds(0, 384)
+    right = pl.ds(384, 384)
     sa = {}
     sb = {}
 
@@ -246,28 +248,56 @@
         g = dot_tn(slope_s[:, k * 128:(k + 1) * 128], img_rows)
         ga = g[:, :H].reshape(4, R, H)
         gb = g[:, H:].reshape(4, R, H)
-        if k:
-            a_send[k - 1] = ga.astype(BF)
-            sa[k] = copy(a_send.at[k - 1, 1:], a_rcv.at[3 - k, 1:], dx(k))
+        if k == 2:
+            a_send[1] = ga.astype(BF)
+            sa["far", 1] = copy(a_send.at[1, :, :, left], a_rcv.at[1, :, :, left], dx(1))
+            sa["far", 3] = copy(a_send.at[1, :, :, right], a_rcv.at[1, :, :, right], dx(3))
+        elif k == 1:
+            a_mid[0] = ga[:, :, :384]
+            a_send[0, :, :, right] = ga[:, :, 384:].astype(BF)
+            sa["near", 1] = copy(a_send.at[0, :, :, right], a_rcv.at[0, :, :, right], dx(1))
+        elif k == 3:
+            a_mid[1] = ga[:, :, 384:]
+            a_send[2, :, :, left] = ga[:, :, :384].astype(BF)
+            sa["near", 3] = copy(a_send.at[2, :, :, left], a_rcv.at[2, :, :, left], dx(3))
         else:
             a_own[...] = ga
         b_own[k] = gb[0]
-        b_send[:, k] = gb[1:].astype(BF)
-        for j in (1, 3, 2):
-            sb[j, k] = copy(b_send.at[j - 1, k], b_rcv.at[3 - j, k], dy(j))
-
+        b_send[1, k] = gb[2].astype(BF)
+        sb["far", 1, k] = copy(b_send.at[1, k, :, left], b_rcv.at[1, k, :, left], dy(1))
+        sb["far", 3, k] = copy(b_send.at[1, k, :, right], b_rcv.at[1, k, :, right], dy(3))
+        b_mid[0, k] = gb[1, :, :384]
+        b_mid[1, k] = gb[3, :, 384:]
+        b_send[0, k, :, right] = gb[1, :, 384:].astype(BF)
+        b_send[2, k, :, left] = gb[3, :, :384].astype(BF)
+        sb["near", 1, k] = copy(b_send.at[0, k, :, right], b_rcv.at[0, k, :, right], dy(1))
+        sb["near", 3, k] = copy(b_send.at[2, k, :, left], b_rcv.at[2, k, :, left], dy(3))
+
+    def relay_a():
+        for way, mid, cols in ((1, 0, left), (3, 1, right)):
+            sa["far", way].wait_recv()
+            a_send[way - 1, :, :, cols] = (a_mid[mid] + a_rcv[1, :, :, cols].astype(F32)).astype(BF)
+            sa["sum", way] = copy(a_send.at[way - 1, 1:, :, cols], a_rcv.at[way - 1, 1:, :, cols], dx(way))
+        for way, cols in ((1, left), (3, right)):
+            sa["own", way] = copy(a_send.at[way - 1, 0, :, cols], a_rcv.at[way - 1, 0, :, cols], dx(way))
+
+    def relay_b(k):
+        for way, mid, cols in ((1, 0, left), (3, 1, right)):
+            sb["far", way, k].wait_recv()
+            b_send[way - 1, k, :, cols] = (b_mid[mid, k] + b_rcv[1, k, :, cols].astype(F32)).astype(BF)
+            sb["sum", way, k] = copy(b_send.at[way - 1, k, :, cols], b_rcv.at[way - 1, k, :, cols], dy(way))
+
+    text_grads(2)
     text_grads(1)
-    text_grads(3)
     ci_send[...] = jnp.dot(
         slope_s[8 * R:, :], txt_rows, preferred_element_type=F32
     ).astype(BF).reshape(8, R, E)
     ci_copy = copy(ci_send, ci_rcv, other)
-    text_grads(2)
+    text_grads(3)
     text_grads(0)
-    for k in (1, 3, 2):
-        sa[k, 0] = copy(a_send.at[k - 1, 0], a_rcv.at[3 - k, 0], dx(k))
-
+    relay_b(2)
     pi_own[...] = jnp.dot(slope_s[:8 * R, :], txt_rows, preferred_element_type=F32).reshape(8, R, E)
+    relay_b(1)
 
     part = jnp.sum(acc)
     lx[0] = jnp.full((8, 128), part, F32)
@@ -302,25 +332,33 @@
             rzm[step - 1, r].wait_recv()
             send_m(step, r, pi_own[4 + step, :, parts[r]] + zm_rcv[step - 1, :, parts[r]].astype(F32))
 
+    relay_a()
+    relay_b(3)
+    relay_b(0)
     ring(1)
 
-    def summed(own, got):
-        return own + got[0].astype(F32) + got[1].astype(F32) + got[2].astype(F32)
-
-    for k in (1, 2, 3):
-        sa[k].wait_recv()
-    a2_send[...] = summed(a_own[1:], [a_rcv[k, 1:] for k in range(3)]).astype(BF)
+    def summed(own, *got):
+        for part in got:
+            own = own + part.astype(F32)
+        return own
+
+    for way in (1, 3):
+        sa["near", way].wait_recv()
+        sa["sum", way].wait_recv()
+    a2_send[...] = summed(a_own[1:], a_rcv[0, 1:], a_rcv[2, 1:]).astype(BF)
     a2 = [copy(a2_send.at[k - 1], a2_rcv.at[3 - k], dy(k)) for k in (1, 2, 3)]
-    for k in (1, 2, 3):
-        for j in (1, 2, 3):
-            sb[j, k].wait_recv()
-    b2_send[...] = summed(b_own[1:], [b_rcv[k, 1:] for k in range(3)]).astype(BF)
+    for way in (1, 3):
+        for k in (1, 2, 3):
+            sb["near", way, k].wait_recv()
+            sb["sum", way, k].wait_recv()
+    b2_send[...] = summed(b_own[1:], b_rcv[0, 1:], b_rcv[2, 1:]).astype(BF)
     b2 = [copy(b2_send.at[k - 1], b2_rcv.at[3 - k], dx(k)) for k in (1, 2, 3)]
-    for k in (1, 2, 3):
-        sa[k, 0].wait_recv()
-        sb[k, 0].wait_recv()
-    ga0 = summed(a_own[0], [a_rcv[k, 0] for k in range(3)])
-    gb0 = summed(b_own[0], [b_rcv[k, 0] for k in range(3)])
+    for way in (1, 3):
+        sa["own", way].wait_recv()
+        sb["near", way, 0].wait_recv()
+        sb["sum", way, 0].wait_recv()
+    ga0 = summed(a_own[0], a_rcv[0, 0], a_rcv[2, 0])
+    gb0 = summed(b_own[0], b_rcv[0, 0], b_rcv[2, 0])
 
     for cp in lxc:
         cp.wait_recv()
@@ -334,8 +372,8 @@
         cp.wait_recv()
     for cp in b2:
         cp.wait_recv()
-    ga0 = summed(ga0, a2_rcv)
-    gb0 = summed(gb0, b2_rcv)
+    ga0 = summed(ga0, a2_rcv[0], a2_rcv[1], a2_rcv[2])
+    gb0 = summed(gb0, b2_rcv[0], b2_rcv[1], b2_rcv[2])
 
     def back(m, ga, gb):
         ua = full[m, :, A]
@@ -406,8 +444,6 @@
     lax.fori_loop(0, 16, cut, 0, unroll=4)
     cw = copy(cw_send, cw_rcv, other)
 
-    pg_img.wait_recv()
-    fg_img = feature_terms(0, w_img, fi_send, fi_rcv)
     lcc.wait_recv()
     lz[0] = lc[0] + lc[1]
     lzc = [copy(lz.at[0], lz.at[8 - k], dz(k)) for k in range(1, 8)]
@@ -426,6 +462,8 @@
         if k:
             zw.append(copy(s2.at[yl * 8 + zz], zw_rcv.at[0, 8 - k], dz(k)))
 
+    pg_img.wait_recv()
+    fg_img = feature_terms(0, w_img, fi_send, fi_rcv)
     txt_out[...] = dot_nt(pg64[1], w_txt[my_feat, :])
     img_out[...] = dot_nt(pg64[0], w_img[my_feat, :])
 
@@ -445,7 +483,8 @@
     wg_out[:, pl.ds(pl.multiple_of(384 * yl, 128), 384)] = near[:11, :]
     wg_out[:, pl.ds(pl.multiple_of(384 * (1 - yl), 128), 384)] = far[:11, :]
     fg_img.wait_recv()
-    img_out[...] += fi_rcv[...]
+    img_out[...] += fi_rcv[...].astype(F32)
+    assert counter[0] <= N_SEM
     for cp in sent:
         cp.wait_send()
 
@@ -475,11 +514,12 @@
             V((64, FEAT), BF), V((64, FEAT), BF), V((FEAT, H), BF), V((FEAT, H), BF),
             V((2, 64, H), F32), V((2, R, H), F32), V((2, R, E), F32), V((2, R, 128), F32),
             V((4, 4, R, E), BF), V((2, 8, R, E), BF), V((16 * R, 16 * R), BF), V((4, 4, R, 512), BF), V((2, R, FEAT), BF),
+            V((2, 4, R, 384), F32), V((2, 4, R, 384), F32),
             V((3, 4, R, H), BF), V((3, 4, R, H), BF), V((4, R, H), F32), V((3, R, H), BF), V((3, R, H), BF),
             V((3, 4, R, H), BF), V((3, 4, R, H), BF), V((4, R, H), F32), V((3, R, H), BF), V((3, R, H), BF),
             V((8, R, E), BF), V((8, R, E), BF), V((8, R, E), F32),
             V((4, R, E), BF), V((4, R, E), BF), V((4, R, E), BF), V((4, R, E), BF),
-            V((2, R, E), BF), V((2, 64, H), BF), V((4, 4, R, 384), BF), V((64, FH), F32), V((64, FH), F32), V((64, FH), BF), V((64, FH), BF),
+            V((2, R, E), BF), V((2, 64, H), BF), V((4, 4, R, 384), BF), V((64, FH), BF), V((64, FH), BF), V((64, FH), BF), V((64, FH), BF),
             V((528, 384), F32), V((16, 16, 384), BF), V((16, 16, 384), BF), V((16, 16, 384), BF), V((2, 8, 16, 384), BF),
             V((4, 8, 128), F32), V((4, 8, 128), F32), V((2, 8, 128), F32), V((8, 8, 128), F32),
             V((16 * R, 16 * R), F32),

time: 74.6 us -> 73.6 us (0.987)
  Pallas kernels: 72.6 us -> 71.5 us
    pallas_call x1, Pallas kernels: 70.1 us -> 69.1 us  [body(): pl.pallas_call(kernel, out_shape=(jax.ShapeDtypeStruct((1,), F32), jax.Sh...]
where the time goes in v4:
time: 73.6 us; the launch traced here: 73.5 us
  Pallas kernels  71.5 us (97%)
  between operations  1.93 us (3%)
    pallas_call x1, Pallas kernels, body(): pl.pallas_call(kernel, out_shape=(jax.ShapeDtypeStruct((1,), F32), jax.Sh...  69.1 us
    pallas_call x1, Pallas kernels, body(): pl.pallas_call(hand_out, out_shape=tuple((jax.ShapeDtypeStruct(r.shape, r...  2.48 us

profile of v4, /device:TPU:1, one launch (start us, length us, event | category | flops | bytes accessed | tf_op | source)
XLA Modules:
  0.0 73.5 jit_solution(10636521844160226319)
XLA Ops:
  1.9 69.1 %fused.1 = (f32[1]{0:T(128)}, f32[64,704]{1,0:T(8,128)}, f32[64,704]{1,0:T(8,128)}, f32[11,768]{1,0:T(8,128)}) custom-call(f32[1,1]{1,0:T(1,128)} %bitcast.3.scale_ref, f32[1,1]{1,0:T(1,128)} %bitcast.4.bias_ref, bf16[64,1408]{1,0:T(8,128)(2,1)} %img_f_hbm.1, bf16[64,1408]{1,0:T(8,128)(2,1)} %txt_f_hbm.1, bf16[1408,768]{1,0:T(8,128)(2,1)} %img_w_hbm.1, ...), custom_call_target="tpu_custom_call" | custom-call | tf_op jit(solution)/shard_map/fused/pallas_call | solution.py:503
  71.0 2.5 %hand_out.1 = (f32[1]{0:T(128)}, f32[64,704]{1,0:T(8,128)}, f32[64,704]{1,0:T(8,128)}, f32[11,768]{1,0:T(8,128)}) custom-call(f32[1]{0:T(128)} %get-tuple-element.12.refs_0_, f32[64,704]{1,0:T(8,128)} %get-tuple-element.13.refs_1_, f32[64,704]{1,0:T(8,128)} %get-tuple-element.14.refs_2_, f32[11,768]{1,0:T(8,128)} %get-tuple-element.15.refs_3_), custom_call_target="tpu_custom_call" | custom-call | tf_op jit(solution)/shard_map/hand_out/pallas_call | solution.py:535

commit v5 on v4

--- a/solution.py
+++ b/solution.py
@@ -83,14 +83,19 @@
 
     sent = []
 
+    def flush(upto):
+        for cp in sent[:upto]:
+            cp.wait_send()
+        del sent[:upto]
+
     loads = [
         pltpu.make_async_copy(img_f_hbm, img_feat, wsem.at[0]),
         pltpu.make_async_copy(img_w_hbm, w_img, wsem.at[1]),
         pltpu.make_async_copy(txt_f_hbm, txt_feat, wsem.at[2]),
         pltpu.make_async_copy(txt_w_hbm, w_txt, wsem.at[3]),
     ]
-    for load in loads:
-        load.start()
+    loads[1].start()
+    loads[0].start()
 
     barrier = pltpu.get_barrier_semaphore()
     partners = [dx(k) for k in (1, 2, 3)] + [dy(k) for k in (1, 2, 3)]
@@ -107,6 +112,8 @@
         return pl.ds(pl.multiple_of(256 * x_ + 128 * (x_ // 2), 128), 512)
 
     loads[0].wait()
+    loads[3].start()
+    loads[2].start()
     loads[1].wait()
     proj[0] = jnp.dot(img_feat[...], w_img[...], preferred_element_type=F32)
     pl.semaphore_wait(barrier, len(partners))
@@ -186,8 +193,10 @@
             zm[step, q].wait_recv()
             if step < 3 or q >= 2:
                 zm[step + 1, q] = copy(img_all.at[0, step, :, part], img_all.at[0, step + 1, :, part], dz(7))
-        cf[8 - step] = copy(img_all.at[0, 8 - step], img_all.at[1, 8 - step], other)
-        cf[step] = copy(img_all.at[0, step], img_all.at[1, step], other)
+            if q % 2:
+                cols = (A, B)[q // 2]
+                for slot in (8 - step, step):
+                    cf[slot, q] = copy(img_all.at[0, slot, :, cols], img_all.at[1, slot, :, cols], other)
 
     along_z(1)
     second(1)
@@ -195,10 +204,10 @@
     along_z(2)
     second(2)
     along_z(3)
-    for q in (0, 1):
-        zp[4, q].wait_recv()
-        zm[4, q + 2].wait_recv()
-    cf[4] = copy(img_all.at[0, 4], img_all.at[1, 4], other)
+    for way, cols, q in ((zp, A, 0), (zm, B, 2)):
+        way[4, q].wait_recv()
+        way[4, q + 1].wait_recv()
+        cf[4, q] = copy(img_all.at[0, 4, :, cols], img_all.at[1, 4, :, cols], other)
     for s in range(4):
         for j in (1, 2, 3):
             ay[s, j].wait_recv()
@@ -233,8 +242,8 @@
     logit_s[0:8 * R, :] = dot_nt(img_all[0].reshape(8 * R, E), txt_rows)
     acc = strip(0, jnp.zeros((8, 16 * R), F32), True)
     acc = lax.fori_loop(1, 8, lambda i, a: strip(i, a, False), acc, unroll=True)
-    for s in range(8):
-        cf[s].wait_recv()
+    for cp in cf.values():
+        cp.wait_recv()
     logit_s[8 * R:, :] = dot_nt(img_all[1].reshape(8 * R, E), txt_rows)
     acc = lax.fori_loop(8, 16, lambda i, a: strip(i, a, False), acc, unroll=4)
     img_rows = img_all[...].reshape(16 * R, E)
@@ -388,6 +397,7 @@
         pg64[m, mine, :] = pgf[m, :, my_cols]
         return cp
 
+    before = len(sent)
     back(1, ga0, gb0)
     pg_txt = share(1)
 
@@ -425,6 +435,7 @@
     lcc = copy(lc.at[0], lc.at[1], other)
     for cp in fw:
         cp.wait_recv()
+    flush(before)
     for cp in pp:
         cp.wait_recv()
     wg[0:512, :] = dot_tn(feat_win[...].reshape(16 * R, 512), pg_plane[...].reshape(16 * R, 384))
@@ -455,6 +466,7 @@
         return carry
 
     lax.fori_loop(0, 16, add_core, 0, unroll=4)
+    before = len(sent)
     zw = []
     for k in (4, 3, 5, 2, 6, 1, 7, 0):
         zz = lax.rem(z + k, 8)
@@ -474,6 +486,7 @@
         cp.wait_recv()
     total = ((lz[0] + lz[4]) + (lz[2] + lz[6])) + ((lz[1] + lz[5]) + (lz[3] + lz[7]))
     loss_out[0] = jnp.max(total) / 8192.0
+    flush(before)
     for cp in zw:
         cp.wait_recv()
     far = zw_rcv[1, 0].astype(F32)

time: 73.6 us -> 73 us (level)
  no operation moved by 1% of the time
where the time goes in v5:
time: 73 us; the launch traced here: 72.8 us
  Pallas kernels  70.8 us (97%)
  between operations  1.93 us (3%)
    pallas_call x1, Pallas kernels, body(): pl.pallas_call(kernel, out_shape=(jax.ShapeDtypeStruct((1,), F32), jax.Sh...  68.4 us
    pallas_call x1, Pallas kernels, body(): pl.pallas_call(hand_out, out_shape=tuple((jax.ShapeDtypeStruct(r.shape, r...  2.48 us

profile of v5, /device:TPU:1, one launch (start us, length us, event | category | flops | bytes accessed | tf_op | source)
XLA Modules:
  0.0 72.8 jit_solution(16858939253780295353)
XLA Ops:
  1.9 68.4 %fused.1 = (f32[1]{0:T(128)}, f32[64,704]{1,0:T(8,128)}, f32[64,704]{1,0:T(8,128)}, f32[11,768]{1,0:T(8,128)}) custom-call(f32[1,1]{1,0:T(1,128)} %bitcast.3.scale_ref, f32[1,1]{1,0:T(1,128)} %bitcast.4.bias_ref, bf16[64,1408]{1,0:T(8,128)(2,1)} %img_f_hbm.1, bf16[64,1408]{1,0:T(8,128)(2,1)} %txt_f_hbm.1, bf16[1408,768]{1,0:T(8,128)(2,1)} %img_w_hbm.1, ...), custom_call_target="tpu_custom_call" | custom-call | tf_op jit(solution)/shard_map/fused/pallas_call | solution.py:516
  70.3 2.5 %hand_out.1 = (f32[1]{0:T(128)}, f32[64,704]{1,0:T(8,128)}, f32[64,704]{1,0:T(8,128)}, f32[11,768]{1,0:T(8,128)}) custom-call(f32[1]{0:T(128)} %get-tuple-element.12.refs_0_, f32[64,704]{1,0:T(8,128)} %get-tuple-element.13.refs_1_, f32[64,704]{1,0:T(8,128)} %get-tuple-element.14.refs_2_, f32[11,768]{1,0:T(8,128)} %get-tuple-element.15.refs_3_), custom_call_target="tpu_custom_call" | custom-call | tf_op jit(solution)/shard_map/hand_out/pallas_call | solution.py:548

commit v6 on v5

--- a/solution.py
+++ b/solution.py
@@ -115,9 +115,12 @@
     loads[3].start()
     loads[2].start()
     loads[1].wait()
-    proj[0] = jnp.dot(img_feat[...], w_img[...], preferred_element_type=F32)
-    pl.semaphore_wait(barrier, len(partners))
-    swap_img = copy(proj.at[0, theirs], proj_rcv.at[0], fs_partner)
+    swap_img = []
+    for cols in (pl.ds(0, 384), pl.ds(384, 384)):
+        proj[0, :, cols] = jnp.dot(img_feat[...], w_img[:, cols], preferred_element_type=F32)
+        if not swap_img:
+            pl.semaphore_wait(barrier, len(partners))
+        swap_img.append(copy(proj.at[0, theirs, cols], proj_rcv.at[0, :, cols], fs_partner))
     loads[2].wait()
     loads[3].wait()
     proj[1] = jnp.dot(txt_feat[...], w_txt[...], preferred_element_type=F32)
@@ -156,7 +159,8 @@
     zm = {}
     cf = {}
 
-    swap_img.wait_recv()
+    for cp in swap_img:
+        cp.wait_recv()
     img_all[0, 0] = embed(0)
     parts = [pl.ds(384 * q, 384) for q in range(4)]
     for q, part in enumerate(parts):

time: 73 us -> 72.9 us (level)
  no operation moved by 1% of the time
where the time goes in v6:
time: 72.9 us; the launch traced here: 72.7 us
  Pallas kernels  70.7 us (97%)
  between operations  1.93 us (3%)
    pallas_call x1, Pallas kernels, body(): pl.pallas_call(kernel, out_shape=(jax.ShapeDtypeStruct((1,), F32), jax.Sh...  68.3 us
    pallas_call x1, Pallas kernels, body(): pl.pallas_call(hand_out, out_shape=tuple((jax.ShapeDtypeStruct(r.shape, r...  2.48 us

profile of v6, /device:TPU:1, one launch (start us, length us, event | category | flops | bytes accessed | tf_op | source)
XLA Modules:
  0.0 72.7 jit_solution(6983917222978143500)
XLA Ops:
  1.9 68.3 %fused.1 = (f32[1]{0:T(128)}, f32[64,704]{1,0:T(8,128)}, f32[64,704]{1,0:T(8,128)}, f32[11,768]{1,0:T(8,128)}) custom-call(f32[1,1]{1,0:T(1,128)} %bitcast.3.scale_ref, f32[1,1]{1,0:T(1,128)} %bitcast.4.bias_ref, bf16[64,1408]{1,0:T(8,128)(2,1)} %img_f_hbm.1, bf16[64,1408]{1,0:T(8,128)(2,1)} %txt_f_hbm.1, bf16[1408,768]{1,0:T(8,128)(2,1)} %img_w_hbm.1, ...), custom_call_target="tpu_custom_call" | custom-call | tf_op jit(solution)/shard_map/fused/pallas_call | solution.py:520
  70.2 2.5 %hand_out.1 = (f32[1]{0:T(128)}, f32[64,704]{1,0:T(8,128)}, f32[64,704]{1,0:T(8,128)}, f32[11,768]{1,0:T(8,128)}) custom-call(f32[1]{0:T(128)} %get-tuple-element.12.refs_0_, f32[64,704]{1,0:T(8,128)} %get-tuple-element.13.refs_1_, f32[64,704]{1,0:T(8,128)} %get-tuple-element.14.refs_2_, f32[11,768]{1,0:T(8,128)} %get-tuple-element.15.refs_3_), custom_call_target="tpu_custom_call" | custom-call | tf_op jit(solution)/shard_map/hand_out/pallas_call | solution.py:552
